TPU v7x, 1024 devices: a whole 4x8x16 slice. The times are simulated.
1024 devices in a mesh: blk: 256 (over y_lo, x, z, core), aux: 4 (over y_hi).
Axes of the slice: x: 4, y: 8 (y_hi: 4, y_lo: 2; y = y_hi * 2 + y_lo), z: 16, core: 2. Of those that a mesh axis runs over, the one named last changes fastest.
Arguments:
- factor: bfloat16 [2048, 16, 704], P(('blk', 'aux')), may hold values from -0.125 to 0.125
- amplitude_forward: bfloat16 [256, 3072, 1024], P('blk', 'aux'), may hold values from -6 to 6
- amplitude_reversed: bfloat16 [256, 3072, 1024], P('blk', 'aux'), may hold values from -6 to 6
- block_map: int32 [256, 2], P('blk'), may hold values from 0 to 21, as said below
- pair_list: int32 [3072, 2], P('aux'), may hold values from 0 to 63, as said below
- virt_energy: float32 [16], replicated, may hold values from 0.5 to 3
- occ_energy: float32 [64], replicated, may hold values from -3 to -0.5
Outputs:
- update: float32 [4, 196608], P('aux', 'blk')
Inputs may be any that keep to these rules, and one draw needn't show every extreme that they name: `block_map`: each row holds two different block numbers below 22; no two rows are equal. `pair_list`: no two rows are equal.
All inputs are finite; a program needn't handle non-finite values.
Results may differ from a plain program's by a relative error of at most 0.0029.
Values may be sent and summed in bfloat16 or wider, within the bound.
No kernel may reach another device: no remote copies, remote signals or barrier semaphores. Data moves between devices by JAX's collectives and lax.ppermute only.
A program may use at most 64 MiB of HBM per device.

v0:
```python
import jax
import jax.numpy as jnp
from jax import lax
from jax.sharding import PartitionSpec as P

AW = 16
BLOCK_VIRTUALS = 32


def pick_blocks(shard_piece, first_block, second):
    left_part = lax.dynamic_slice_in_dim(shard_piece, first_block, BLOCK_VIRTUALS, 2)
    right_part = lax.dynamic_slice_in_dim(shard_piece, second, BLOCK_VIRTUALS, 2)
    return jnp.concatenate([left_part, right_part], axis=2)


def cross_products(picked):
    row_count = picked.shape[0]
    left_slab = picked[:, :, :BLOCK_VIRTUALS].reshape(row_count, AW * BLOCK_VIRTUALS)
    right_slab = picked[:, :, BLOCK_VIRTUALS:].reshape(row_count, AW * BLOCK_VIRTUALS)
    return lax.dot_general(
        left_slab, right_slab, (((0,), (0,)), ((), ())), preferred_element_type=jnp.float32
    )


def table_lookup(index_list, table):
    slots_here = jnp.arange(table.shape[0], dtype=jnp.int32)
    return jnp.sum(
        jnp.where(index_list[:, None] == slots_here[None, :], table[None, :], 0.0), axis=1
    )


def shards(
    factor, amplitude_forward, amplitude_reversed, block_map, pair_list, virt_energy, occ_energy
):
    first_block = block_map[0, 0] * BLOCK_VIRTUALS
    second = block_map[0, 1] * BLOCK_VIRTUALS
    gathered = lax.all_gather(factor, "blk", axis=0, tiled=True)
    partial_sum = cross_products(pick_blocks(gathered, first_block, second))
    coulomb = lax.psum(partial_sum, "aux")
    weights = (
        coulomb.reshape(AW, BLOCK_VIRTUALS, AW, BLOCK_VIRTUALS)
        .transpose(0, 2, 1, 3)
        .reshape(AW * AW, BLOCK_VIRTUALS * BLOCK_VIRTUALS)
        .astype(jnp.bfloat16)
    )
    direct_term = lax.dot_general(
        amplitude_forward[0], weights, (((1,), (1,)), ((), ())), preferred_element_type=jnp.float32
    )
    swapped = lax.dot_general(
        amplitude_reversed[0], weights, (((1,), (1,)), ((), ())), preferred_element_type=jnp.float32
    )
    swapped = swapped.reshape(-1, AW, AW).transpose(0, 2, 1).reshape(-1, AW * AW)
    slot_term = (direct_term + swapped).reshape(-1)
    owned = lax.psum_scatter(slot_term, "blk", scatter_dimension=0, tiled=True)
    owned_len = owned.shape[0]
    offset = lax.axis_index("blk") * owned_len
    flat_index = offset + jnp.arange(owned_len, dtype=jnp.int32)
    pair_at = flat_index // (AW * AW)
    cell_index = flat_index % (AW * AW)
    pair_energy = table_lookup(pair_list[:, 0], occ_energy) + table_lookup(
        pair_list[:, 1], occ_energy
    )
    owned_pair = table_lookup(pair_at, pair_energy)
    energy_a = table_lookup(cell_index // AW, virt_energy)
    energy_b = table_lookup(cell_index % AW, virt_energy)
    denominator = owned_pair - energy_a - energy_b
    return (owned / denominator).reshape(1, owned_len)


def solution(mesh):
    placed = (
        P(("blk", "aux"), None, None),
        P("blk", "aux", None),
        P("blk", "aux", None),
        P("blk", None),
        P("aux", None),
        P(),
        P(),
    )
    return jax.shard_map(
        shards, mesh=mesh, in_specs=placed, out_specs=P("aux", "blk"), check_vma=False
    )
```

profile of v0, /device:TPU:1, one launch (start us, length us, event | category | flops | bytes accessed | tf_op | source)
XLA Modules:
  0.0 2485.2 jit_solution(11945844869664482281)
XLA Ops:
  6.5 0.7 all-gather.2.cloned.1.call-update
  7.3 1.3 fusion.17
  9.9 443.6 %all-gather.2.cloned.1.call-done = bf16[512,16,704]{2,1,0:T(8,128)(2,1)} async-done(((bf16[2,16,704]{2,1,0:T(8,128)(2,1)}), bf16[512,16,704]{2,1,0:T(8,128)(2,1)}) %all-gather.2.cloned.1.call-update) | async-done | bytes 11534352 | tf_op jit(solution)/shard_map/all_gather | solution.py:37
  453.5 5.4 constant_dynamic-slice_fusion
  458.9 2.5 copy.23
  461.4 3.2 copy.24
  464.6 1.5 fusion.18
  466.1 45.1 %all-reduce.5 = bf16[512,512]{1,0:T(8,128)(2,1)S(1)} all-reduce(f32[512,512]{1,0:T(8,128)S(1)} %fusion.18), channel_id=1, replica_groups=mesh['blk'=256,'aux'=4] {'aux'}, use_global_device_ids=true, to_apply=%region_0.0 | all-reduce | flops 262144 | bytes 1572864 | tf_op jit(solution)/shard_map/psum | solution.py:39
  511.2 2.2 convert_element_type.14
  513.4 3.4 copy.27
  516.9 3.5 convert_element_type.16
  520.4 0.6 fusion
  521.0 0.5 copy.21
  521.5 0.3 copy-done.1
  521.8 0.6 fusion.7
  522.5 1.2 copy.22
  523.7 2.4 copy.25
  526.2 0.1 select_reduce_fusion.1
  526.3 1.3 dynamic-slice
  528.3 0.1 select_reduce_fusion.4
  528.4 0.5 select_reduce_fusion
  528.9 1948.1 %all-reduce.4.cloned.1.call-done = f32[196608]{0:T(1024)} async-done(((f32[196608]{0:T(1024)}), f32[196608]{0:T(1024)}) %all-reduce.4.cloned.1.call-update) | async-done | bytes 786448
  2477.0 0.8 dynamic-slice_divide_fusion
  2477.8 0.6 reshape.99
  (16 shorter events, 0.1 us)
Async XLA Ops:
  6.5 513.9 %copy-start = (bf16[1,768,1024]{2,1,0:T(8,128)(2,1)S(1)}, bf16[1,768,1024]{2,1,0:T(8,128)(2,1)}, u32[]{:S(2)}) copy-start(bf16[1,768,1024]{2,1,0:T(8,128)(2,1)} %param.9) | copy-start | bytes 4718596
  6.5 447.0 %all-gather.2.cloned.1.call-start = ((), (), s32[]{:S(2)}) async-start(), calls=%async_computation | async-start | bytes 12632064 | tf_op jit(solution)/shard_map/all_gather | solution.py:37
  7.3 2469.7 %all-reduce.4.cloned.1.call-start = ((), (), s32[]{:S(2)}) async-start(), calls=%async_computation.1 | async-start | bytes 1572864
  520.4 1.4 copy-start.1
  522.5 3.7 copy-start.2
  522.5 3.7 copy-start.3
  522.5 5.8 copy-start.4
Sparse Core Ops, SparseCore 0:
  10.1 443.3 all-gather.1
  526.2 1950.7 all-reduce.3
where the time goes:
time: 2490 us
  waiting for transfers between devices  2390 us (96%)
  blocking collectives  45.1 us (2%)
  local copies, waits for them, and re-layouts  27.9 us (1%)
    unnamed x3, waiting for transfers between devices  1950 us
    all_gather x1, waiting for transfers between devices, shards(): gathered = lax.all_gather(factor, 'blk', axis=0, tiled=True)  444 us
  transfers between devices with their start and end apart: 2, of which 2 were waited for; matrix products, arithmetic and copies ran while one was open for 0% of the time, Pallas kernels for 0%

commit v1 on v0

v1 whole, which is shorter than its diff:
```python
import jax
import jax.numpy as jnp
from jax import lax
from jax.sharding import Mesh
from jax.sharding import PartitionSpec as P

AW = 16
BLOCK_VIRTUALS = 32
NV = 704
BLK = ("yl", "x", "z", "core")
PLANE = ("yl", "x", "core")


def table_lookup(index_list, table):
    slots_here = jnp.arange(table.shape[0], dtype=jnp.int32)
    return jnp.sum(
        jnp.where(index_list[:, None] == slots_here[None, :], table[None, :], 0.0), axis=1
    )


def one_hot_rows(columns, width):
    cols = lax.broadcasted_iota(jnp.int32, (columns.shape[0], width), 1)
    return (columns[:, None] == cols).astype(jnp.bfloat16)


def select_rows(hot, rows):
    return lax.dot_general(
        hot, rows, (((1,), (1,)), ((), ())), preferred_element_type=jnp.float32
    ).astype(jnp.bfloat16)


def shards(
    factor, amplitude_forward, amplitude_reversed, block_map, pair_list, virt_energy, occ_energy
):
    plane_map = lax.all_gather(block_map, PLANE, axis=0, tiled=True)
    line = lax.all_gather(factor, "z", axis=0, tiled=True)
    q_line = line.shape[0]
    wanted = (
        plane_map.reshape(-1, 1) * BLOCK_VIRTUALS + jnp.arange(BLOCK_VIRTUALS, dtype=jnp.int32)
    ).reshape(-1)
    line = line.transpose(1, 0, 2).reshape(AW * q_line, NV)
    picked = select_rows(one_hot_rows(wanted, NV), line)
    picked = picked.reshape(16, 2 * BLOCK_VIRTUALS, AW * q_line)
    picked = lax.all_to_all(picked, PLANE, 0, 0, tiled=True)
    picked = picked.reshape(16, 2, BLOCK_VIRTUALS, AW, q_line)
    partial_sum = jnp.einsum(
        "scaq,sdbq->acbd", picked[:, 0], picked[:, 1], preferred_element_type=jnp.float32
    )
    partial_sum = partial_sum.reshape(4, 4 * BLOCK_VIRTUALS, AW * BLOCK_VIRTUALS)
    quarters = lax.all_to_all(partial_sum, "yh", 0, 0, tiled=True)
    coulomb = quarters[0] + quarters[1] + quarters[2] + quarters[3]
    weights = (
        coulomb.astype(jnp.bfloat16)
        .reshape(4, BLOCK_VIRTUALS, AW, BLOCK_VIRTUALS)
        .transpose(0, 2, 1, 3)
        .reshape(4 * AW, BLOCK_VIRTUALS * BLOCK_VIRTUALS)
    )
    weights = lax.all_gather(weights, "yh", axis=0, tiled=True)
    mirrored = (
        weights.reshape(AW, AW, -1).transpose(1, 0, 2).reshape(AW * AW, -1)
    )
    direct_term = lax.dot_general(
        amplitude_forward[0], weights, (((1,), (1,)), ((), ())), preferred_element_type=jnp.float32
    )
    swapped = lax.dot_general(
        amplitude_reversed[0], mirrored, (((1,), (1,)), ((), ())), preferred_element_type=jnp.float32
    )
    slot_term = (direct_term + swapped).astype(jnp.bfloat16)
    row = jnp.arange(768, dtype=jnp.int32)
    source = jnp.arange(768, dtype=jnp.int32).reshape(8, 16, 2, 3).transpose(0, 2, 1, 3).reshape(-1)
    hot = one_hot_rows(source, 768)
    ordered = lax.dot_general(
        hot, slot_term, (((1,), (0,)), ((), ())), preferred_element_type=jnp.float32
    ).astype(jnp.bfloat16)
    ordered = lax.all_to_all(ordered.reshape(16, 48, 256), PLANE, 0, 0, tiled=True)
    plane_sum = jnp.sum(ordered.astype(jnp.float32), axis=0).reshape(16, 768)
    owned = jnp.sum(lax.all_to_all(plane_sum, "z", 0, 0, tiled=True), axis=0)

    owned_len = owned.shape[0]
    offset = lax.axis_index(BLK) * owned_len
    flat_index = offset + jnp.arange(owned_len, dtype=jnp.int32)
    pair_at = flat_index // (AW * AW)
    cell_index = flat_index % (AW * AW)
    pair_energy = table_lookup(pair_list[:, 0], occ_energy) + table_lookup(
        pair_list[:, 1], occ_energy
    )
    owned_pair = table_lookup(pair_at, pair_energy)
    energy_a = table_lookup(cell_index // AW, virt_energy)
    energy_b = table_lookup(cell_index % AW, virt_energy)
    denominator = owned_pair - energy_a - energy_b
    return (owned / denominator).reshape(1, owned_len)


def solution(mesh):
    fine = Mesh(mesh.devices.reshape(2, 4, 16, 2, 4), BLK + ("yh",))
    placed = (
        P(BLK + ("yh",), None, None),
        P(BLK, "yh", None),
        P(BLK, "yh", None),
        P(BLK, None),
        P("yh", None),
        P(),
        P(),
    )
    return jax.shard_map(
        shards, mesh=fine, in_specs=placed, out_specs=P("yh", BLK), check_vma=False
    )
```

time: 2490 us -> 197 us (0.08)
  waiting for transfers between devices: 2390 us -> 37.8 us
  blocking collectives: 45.1 us -> 104 us
    unnamed x3 -> x0, waiting for transfers between devices: 1950 us -> none
    all_gather x1 -> x0, waiting for transfers between devices: 444 us -> none  [shards(): gathered = lax.all_gather(factor, 'blk', axis=0, tiled=True)]
    all_gather x0 -> x3, blocking collectives: none -> 85.9 us  [the longest x1 41 us: shards(): line = lax.all_gather(factor, 'z', axis=0, tiled=True)]
    psum x1 -> x0, blocking collectives: 45.1 us -> none  [shards(): coulomb = lax.psum(partial_sum, 'aux')]
    all_to_all x0 -> x3, waiting for transfers between devices: none -> 37.8 us  [the longest x1 18.6 us: shards(): quarters = lax.all_to_all(partial_sum, 'yh', 0, 0, tiled=True)]
  transfers between devices with their start and end apart: 2 -> 3, of which waited for: 2 -> 3; matrix products, arithmetic and copies ran while one was open for 0% -> 0% of each run, Pallas kernels for 0% -> 0%
where the time goes in v1:
time: 197 us; the launch traced here: 196 us
  blocking collectives  104 us (53%)
  waiting for transfers between devices  37.8 us (19%)
  starting transfers between devices  22.1 us (11%)
  local copies, waits for them, and re-layouts  19.9 us (10%)
  matrix products  11 us (6%)
    all_gather x1, blocking collectives, shards(): line = lax.all_gather(factor, 'z', axis=0, tiled=True)  41 us
    all_gather x1, blocking collectives, shards(): plane_map = lax.all_gather(block_map, PLANE, axis=0, tiled=True)  27.1 us
    all_to_all x1, waiting for transfers between devices, shards(): quarters = lax.all_to_all(partial_sum, 'yh', 0, 0, tiled=True)  18.6 us
    all_to_all x1, blocking collectives, shards(): picked = lax.all_to_all(picked, PLANE, 0, 0, tiled=True)  18.1 us
    all_gather x1, blocking collectives, shards(): weights = lax.all_gather(weights, 'yh', axis=0, tiled=True)  17.7 us
    all_to_all x1, starting transfers between devices, shards(): lax.all_to_all(ordered.reshape(16, 48, 256), PLANE, 0, 0, tiled=True)  12.2 us
    all_to_all x1, waiting for transfers between devices, shards(): owned = jnp.sum(lax.all_to_all(plane_sum, 'z', 0, 0, tiled=True), axis=0)  11.1 us
    all_to_all x1, waiting for transfers between devices, shards(): lax.all_to_all(ordered.reshape(16, 48, 256), PLANE, 0, 0, tiled=True)  8.08 us
  transfers between devices with their start and end apart: 3, of which 3 were waited for; matrix products, arithmetic and copies ran while one was open for 0% of the time, Pallas kernels for 0%

profile of v1, /device:TPU:1, one launch (start us, length us, event | category | flops | bytes accessed | tf_op | source)
XLA Modules:
  0.0 196.1 jit_solution(16171294554530439144)
XLA Ops:
  0.0 41.0 %all_gather.10 = bf16[32,16,704]{2,1,0:T(8,128)(2,1)S(1)} all-gather(bf16[2,16,704]{2,1,0:T(8,128)(2,1)} %param.7), channel_id=1, replica_groups=mesh['yl'=2,'x'=4,'z'=16,'core'=2,'yh'=4] {'z'}, dimensions={0}, use_global_device_ids=true | all-gather | bytes 765952 | tf_op jit(solution)/shard_map/all_gather | solution.py:36
  41.2 27.1 %all-gather = s32[16,1,2]{2,1,0:T(1,128)S(1)} all-gather(s32[1,1,2]{2,1,0:T(1,128)S(1)} %bitcast.54), channel_id=1, replica_groups=mesh['yl'=2,'x'=4,'z'=16,'core'=2,'yh'=4] {'yl','x','core'}, dimensions={0}, use_global_device_ids=true | all-gather | bytes 136 | tf_op jit(solution)/shard_map/all_gather | solution.py:35
  68.6 1.0 fusion.7
  69.7 18.1 %all_to_all.24 = bf16[16,64,512]{2,1,0:T(8,128)(2,1)S(1)} all-to-all(bf16[16,64,512]{2,1,0:T(8,128)(2,1)S(1)} %bitcast.52), channel_id=1, replica_groups=mesh['yl'=2,'x'=4,'z'=16,'core'=2,'yh'=4] {'yl','x','core'}, dimensions={0} | all-to-all | bytes 2097152 | tf_op jit(solution)/shard_map/all_to_all | solution.py:44
  87.8 3.8 %reshape.229 = bf16[16,2,32,16,32]{4,3,2,1,0:T(8,128)(2,1)} reshape(bf16[16,64,512]{2,1,0:T(8,128)(2,1)S(1)} %all_to_all.24) | data formatting | bytes 2097152 | tf_op jit(solution)/shard_map/reshape | solution.py:45
  91.6 3.0 %fusion.26 = (bf16[16,1,32,16,32]{4,3,2,1,0:T(8,128)(2,1)S(1)}, bf16[16,1,32,16,32]{4,3,2,1,0:T(8,128)(2,1)S(1)}) fusion(bf16[16,2,32,16,32]{4,3,2,1,0:T(8,128)(2,1)} %reshape.229), kind=kLoop, calls=%fused_computation.59 | loop fusion | bytes 2097152 | tf_op jit(solution)/shard_map/slice | solution.py:47
  94.6 6.2 %convolution_bitcast_fusion = f32[16,32,16,32]{1,3,0,2:T(8,128)} fusion(bf16[16,1,32,16,32]{4,3,2,1,0:T(8,128)(2,1)S(1)} %get-tuple-element.12, bf16[16,1,32,16,32]{4,3,2,1,0:T(8,128)(2,1)S(1)} %get-tuple-element.11), kind=kOutput, calls=%fused_computation.6 | convolution fusion | flops 268435456 | bytes 2097152 | tf_op jit(solution)/shard_map/scaq,sdbq->acbd/dot_general | solution.py:46
  100.8 5.6 %copy.23 = f32[16,32,16,32]{3,2,1,0:T(8,128)} copy(f32[16,32,16,32]{1,3,0,2:T(8,128)} %convolution_bitcast_fusion) | data formatting | bytes 2097152 | tf_op jit(solution)/shard_map/scaq,sdbq->acbd/transpose | solution.py:46
  106.4 4.4 %reshape.230 = f32[4,128,512]{2,1,0:T(8,128)} reshape(f32[16,32,16,32]{3,2,1,0:T(8,128)} %copy.23) | data formatting | bytes 2097152 | tf_op jit(solution)/shard_map/reshape | solution.py:49
  110.8 5.9 %all-to-all-start.1 = ((f32[4,128,512]{2,1,0:T(8,128)}), f32[4,128,512]{2,1,0:T(8,128)S(1)}, u32[]{:S(2)}, u32[]{:S(2)}) async-start(f32[4,128,512]{2,1,0:T(8,128)} %reshape.230), calls=%async_computation.1 | async-start | bytes 2097152 | tf_op jit(solution)/shard_map/all_to_all | solution.py:50
  116.9 18.6 %all-to-all-done.1 = f32[4,128,512]{2,1,0:T(8,128)S(1)} async-done(((f32[4,128,512]{2,1,0:T(8,128)}), f32[4,128,512]{2,1,0:T(8,128)S(1)}, u32[]{:S(2)}, u32[]{:S(2)}) %all-to-all-start.1) | async-done | bytes 1048608 | tf_op jit(solution)/shard_map/all_to_all | solution.py:50
  135.5 0.3 convert_element_type.24
  136.0 0.5 reshape.231
  136.5 17.7 %all_gather.11 = bf16[256,1024]{1,0:T(8,128)(2,1)S(1)} all-gather(bf16[64,1024]{1,0:T(8,128)(2,1)S(1)} %reshape.231), channel_id=1, replica_groups=mesh['yl'=2,'x'=4,'z'=16,'core'=2,'yh'=4] {'yh'}, dimensions={0}, use_global_device_ids=true | all-gather | bytes 655360 | tf_op jit(solution)/shard_map/all_gather | solution.py:58
  154.3 0.3 copy.25
  154.6 0.6 fusion.2
  155.2 3.2 %fusion.14 = bf16[768,256]{1,0:T(8,128)(2,1)} fusion(f32[256,768]{1,0:T(8,128)S(1)} %fusion.2, bf16[256,1024]{1,0:T(8,128)(2,1)S(1)} %all_gather.11, bf16[1,768,1024]{2,1,0:T(8,128)(2,1)} %param.8, s32[768]{0:T(1024)S(1)} %reshape.226), kind=kOutput, calls=%fused_computation.17 | convolution fusion | flops 705822720 | bytes 3279872 | tf_op jit(solution)/shard_map/dot_general | solution.py:72
  158.5 12.2 %all-to-all-start.2 = ((bf16[16,48,256]{2,1,0:T(8,128)(2,1)}), bf16[16,48,256]{2,1,0:T(8,128)(2,1)S(1)}, u32[]{:S(2)}, u32[]{:S(2)}) async-start(bf16[16,48,256]{2,1,0:T(8,128)(2,1)} %bitcast.18), calls=%async_computation.2 | async-start | bytes 786432 | tf_op jit(solution)/shard_map/all_to_all | solution.py:75
  171.0 8.1 %all-to-all-done.2 = bf16[16,48,256]{2,1,0:T(8,128)(2,1)S(1)} async-done(((bf16[16,48,256]{2,1,0:T(8,128)(2,1)}), bf16[16,48,256]{2,1,0:T(8,128)(2,1)S(1)}, u32[]{:S(2)}, u32[]{:S(2)}) %all-to-all-start.2) | async-done | bytes 393248 | tf_op jit(solution)/shard_map/all_to_all | solution.py:75
  179.1 0.7 all_to_all.18
  179.8 4.0 %all-to-all-start.3 = ((f32[16,1,768]{2,1,0:T(1,128)}), f32[16,1,768]{2,1,0:T(1,128)S(1)}, u32[]{:S(2)}, u32[]{:S(2)}) async-start(f32[16,1,768]{2,1,0:T(1,128)} %all_to_all.18), calls=%async_computation.3 | async-start | bytes 98304 | tf_op jit(solution)/shard_map/all_to_all | solution.py:77
  183.8 0.5 select_reduce_fusion
  184.3 11.1 %all-to-all-done.3 = f32[16,1,768]{2,1,0:T(1,128)S(1)} async-done(((f32[16,1,768]{2,1,0:T(1,128)}), f32[16,1,768]{2,1,0:T(1,128)S(1)}, u32[]{:S(2)}, u32[]{:S(2)}) %all-to-all-start.3) | async-done | bytes 49184 | tf_op jit(solution)/shard_map/all_to_all | solution.py:77
  195.5 0.6 div.44
  (28 shorter events, 1.3 us)
Async XLA Ops:
  0.0 154.6 %copy-start = (bf16[1,768,1024]{2,1,0:T(8,128)(2,1)S(1)}, bf16[1,768,1024]{2,1,0:T(8,128)(2,1)}, u32[]{:S(2)}) copy-start(bf16[1,768,1024]{2,1,0:T(8,128)(2,1)} %param.9) | copy-start | bytes 4718596
  0.0 41.2 %copy-start.2 = (s32[1,2]{1,0:T(1,128)S(1)}, s32[1,2]{1,0:T(1,128)}, u32[]{:S(2)}) copy-start(s32[1,2]{1,0:T(1,128)} %param.10) | copy-start | bytes 28
  110.8 24.7 %all-to-all-start.1 = ((f32[4,128,512]{2,1,0:T(8,128)}), f32[4,128,512]{2,1,0:T(8,128)S(1)}, u32[]{:S(2)}, u32[]{:S(2)}) async-start(f32[4,128,512]{2,1,0:T(8,128)} %reshape.230), calls=%async_computation.1 | async-start | bytes 2097152 | tf_op jit(solution)/shard_map/all_to_all | solution.py:50
  155.2 15.5 %copy-start.1 = (s32[768,2]{0,1:T(2,128)S(1)}, s32[768,2]{0,1:T(2,128)}, u32[]{:S(2)}) copy-start(s32[768,2]{0,1:T(2,128)} %param.11) | copy-start | bytes 18436
  155.2 15.5 %copy-start.3 = (f32[16]{0:T(128)S(1)}, f32[16]{0:T(128)}, u32[]{:S(2)}) copy-start(f32[16]{0:T(128)} %param.12) | copy-start | bytes 196
  155.2 15.6 %copy-start.4 = (f32[64]{0:T(128)S(1)}, f32[64]{0:T(128)}, u32[]{:S(2)}) copy-start(f32[64]{0:T(128)} %param.13) | copy-start | bytes 772
  158.5 20.6 %all-to-all-start.2 = ((bf16[16,48,256]{2,1,0:T(8,128)(2,1)}), bf16[16,48,256]{2,1,0:T(8,128)(2,1)S(1)}, u32[]{:S(2)}, u32[]{:S(2)}) async-start(bf16[16,48,256]{2,1,0:T(8,128)(2,1)} %bitcast.18), calls=%async_computation.2 | async-start | bytes 786432 | tf_op jit(solution)/shard_map/all_to_all | solution.py:75
  179.8 15.7 %all-to-all-start.3 = ((f32[16,1,768]{2,1,0:T(1,128)}), f32[16,1,768]{2,1,0:T(1,128)S(1)}, u32[]{:S(2)}, u32[]{:S(2)}) async-start(f32[16,1,768]{2,1,0:T(1,128)} %all_to_all.18), calls=%async_computation.3 | async-start | bytes 98304 | tf_op jit(solution)/shard_map/all_to_all | solution.py:77

commit v2 on v1

--- a/solution.py
+++ b/solution.py
@@ -1,6 +1,8 @@
 import jax
 import jax.numpy as jnp
 from jax import lax
+from jax.experimental import pallas as pl
+from jax.experimental.pallas import tpu as pltpu
 from jax.sharding import Mesh
 from jax.sharding import PartitionSpec as P
 
@@ -9,6 +11,69 @@
 NV = 704
 BLK = ("yl", "x", "z", "core")
 PLANE = ("yl", "x", "core")
+GROUP = 4
+LANES = 128
+
+
+def swap_lane_blocks(tiles):
+    lane = lax.broadcasted_iota(jnp.int32, tiles[0].shape, 1)
+    block = lax.shift_right_logical(lane, 5)
+    result = []
+    for j in range(GROUP):
+        out = None
+        for i in range(GROUP):
+            shift = (i - j) * BLOCK_VIRTUALS % LANES
+            moved = pltpu.roll(tiles[i], shift, 1) if shift else tiles[i]
+            out = moved if out is None else jnp.where(block == i, moved, out)
+        result.append(out)
+    return result
+
+
+def integrals_kernel(picked_ref, out_ref, left_ref, right_ref, product_ref):
+    for source in range(0, 16, GROUP):
+        for first in range(0, AW, GROUP):
+            lanes = slice(first * BLOCK_VIRTUALS, first * BLOCK_VIRTUALS + LANES)
+            tiles = [
+                picked_ref[source + i, :, lanes].astype(jnp.float32) for i in range(GROUP)
+            ]
+            depth = slice(source * BLOCK_VIRTUALS, source * BLOCK_VIRTUALS + LANES)
+            for j, tile in enumerate(swap_lane_blocks(tiles)):
+                rows = slice((first + j) * BLOCK_VIRTUALS, (first + j + 1) * BLOCK_VIRTUALS)
+                tile = tile.astype(jnp.bfloat16)
+                left_ref[rows, depth] = tile[:BLOCK_VIRTUALS]
+                right_ref[rows, depth] = tile[BLOCK_VIRTUALS:]
+    product_ref[...] = lax.dot_general(
+        left_ref[...],
+        right_ref[...],
+        (((1,), (1,)), ((), ())),
+        preferred_element_type=jnp.float32,
+    ).reshape(product_ref.shape)
+    for c in range(0, BLOCK_VIRTUALS, GROUP):
+        for b in range(0, AW, GROUP):
+            lanes = slice(b * BLOCK_VIRTUALS, b * BLOCK_VIRTUALS + LANES)
+            tiles = [product_ref[:, c + i, lanes] for i in range(GROUP)]
+            for j, tile in enumerate(swap_lane_blocks(tiles)):
+                out_ref[b + j, :, c * BLOCK_VIRTUALS : c * BLOCK_VIRTUALS + LANES] = tile
+
+
+def block_integrals(picked):
+    side = AW * BLOCK_VIRTUALS
+    return pl.pallas_call(
+        integrals_kernel,
+        out_shape=jax.ShapeDtypeStruct((AW, AW, BLOCK_VIRTUALS**2), jnp.float32),
+        in_specs=[pl.BlockSpec(memory_space=pltpu.VMEM)],
+        out_specs=pl.BlockSpec(memory_space=pltpu.VMEM),
+        scratch_shapes=[
+            pltpu.VMEM((side, side), jnp.bfloat16),
+            pltpu.VMEM((side, side), jnp.bfloat16),
+            pltpu.VMEM((AW, BLOCK_VIRTUALS, side), jnp.float32),
+        ],
+        compiler_params=pltpu.CompilerParams(vmem_limit_bytes=24 * 1024 * 1024),
+        cost_estimate=pl.CostEstimate(
+            flops=2 * side**3, bytes_accessed=2 * 1024 * 1024, transcendentals=0
+        ),
+        name="block_integrals",
+    )(picked)
 
 
 def table_lookup(index_list, table):
@@ -32,7 +97,9 @@
 def shards(
     factor, amplitude_forward, amplitude_reversed, block_map, pair_list, virt_energy, occ_energy
 ):
-    plane_map = lax.all_gather(block_map, PLANE, axis=0, tiled=True)
+    plane_map = lax.all_to_all(
+        jnp.broadcast_to(block_map, (16, 2)), PLANE, 0, 0, tiled=True
+    )
     line = lax.all_gather(factor, "z", axis=0, tiled=True)
     q_line = line.shape[0]
     wanted = (
@@ -42,23 +109,11 @@
     picked = select_rows(one_hot_rows(wanted, NV), line)
     picked = picked.reshape(16, 2 * BLOCK_VIRTUALS, AW * q_line)
     picked = lax.all_to_all(picked, PLANE, 0, 0, tiled=True)
-    picked = picked.reshape(16, 2, BLOCK_VIRTUALS, AW, q_line)
-    partial_sum = jnp.einsum(
-        "scaq,sdbq->acbd", picked[:, 0], picked[:, 1], preferred_element_type=jnp.float32
-    )
-    partial_sum = partial_sum.reshape(4, 4 * BLOCK_VIRTUALS, AW * BLOCK_VIRTUALS)
+    partial_sum = block_integrals(picked).reshape(4, 4 * AW, -1)
     quarters = lax.all_to_all(partial_sum, "yh", 0, 0, tiled=True)
     coulomb = quarters[0] + quarters[1] + quarters[2] + quarters[3]
-    weights = (
-        coulomb.astype(jnp.bfloat16)
-        .reshape(4, BLOCK_VIRTUALS, AW, BLOCK_VIRTUALS)
-        .transpose(0, 2, 1, 3)
-        .reshape(4 * AW, BLOCK_VIRTUALS * BLOCK_VIRTUALS)
-    )
-    weights = lax.all_gather(weights, "yh", axis=0, tiled=True)
-    mirrored = (
-        weights.reshape(AW, AW, -1).transpose(1, 0, 2).reshape(AW * AW, -1)
-    )
+    mirrored = lax.all_gather(coulomb.astype(jnp.bfloat16), "yh", axis=0, tiled=True)
+    weights = mirrored.reshape(AW, AW, -1).transpose(1, 0, 2).reshape(AW * AW, -1)
     direct_term = lax.dot_general(
         amplitude_forward[0], weights, (((1,), (1,)), ((), ())), preferred_element_type=jnp.float32
     )

time: 197 us -> 165 us (0.84)
  blocking collectives: 104 us -> 73.2 us
  local copies, waits for them, and re-layouts: 19.9 us -> 3.56 us
  starting transfers between devices: 22.1 us -> 36.3 us
  matrix products: 11 us -> 4.88 us
  waiting for transfers between devices: 37.8 us -> 42.2 us
  Pallas kernels: 0 us -> 3.04 us
    all_gather x2 -> x1, blocking collectives: 44.9 us -> 15.6 us  [shards(): lax.all_gather(coulomb.astype(jnp.bfloat16), 'yh', axis=0, tiled=True)]
    all_to_all x0 -> x1, starting transfers between devices: none -> 17.4 us  [shards(): lax.all_to_all(jnp.broadcast_to(block_map, (16, 2)), PLANE, 0, 0, tiled=T...]
    all_gather x1, blocking collectives: 41 us -> 29.6 us  [shards(): line = lax.all_gather(factor, 'z', axis=0, tiled=True)]
    all_to_all x1, blocking collectives: 18.1 us -> 28.1 us  [shards(): picked = lax.all_to_all(picked, PLANE, 0, 0, tiled=True)]
    reshape x4 -> x0, local copies, waits for them, and re-layouts: 9.01 us -> none  [the longest x1 4.39 us: shards(): partial_sum.reshape(4, 4 * BLOCK_VIRTUALS, AW * BLOCK_VIRTUALS)]
    dot_general x1 -> x0, matrix products: 6.15 us -> none  [shards(): jnp.einsum('scaq,sdbq->acbd', picked[:, 0], picked[:, 1], preferred_eleme...]
    transpose x1, local copies, waits for them, and re-layouts: 5.6 us -> 0.29 us  [shards(): mirrored.reshape(AW, AW, -1).transpose(1, 0, 2).reshape(AW * AW, -1)]
    all_to_all x1, waiting for transfers between devices: 18.6 us -> 23 us  [shards(): quarters = lax.all_to_all(partial_sum, 'yh', 0, 0, tiled=True)]
  transfers between devices with their start and end apart: 3 -> 4, of which waited for: 3 -> 3; matrix products, arithmetic and copies ran while one was open for 0% -> 1% of each run, Pallas kernels for 0% -> 0%
where the time goes in v2:
time: 165 us; the launch traced here: 164 us
  blocking collectives  73.2 us (44%)
  waiting for transfers between devices  42.2 us (26%)
  starting transfers between devices  36.3 us (22%)
  matrix products  4.88 us (3%)
  local copies, waits for them, and re-layouts  3.56 us (2%)
  Pallas kernels  3.04 us (2%)
    all_gather x1, blocking collectives, shards(): line = lax.all_gather(factor, 'z', axis=0, tiled=True)  29.6 us
    all_to_all x1, blocking collectives, shards(): picked = lax.all_to_all(picked, PLANE, 0, 0, tiled=True)  28.1 us
    all_to_all x1, waiting for transfers between devices, shards(): quarters = lax.all_to_all(partial_sum, 'yh', 0, 0, tiled=True)  23 us
    all_to_all x1, starting transfers between devices, shards(): lax.all_to_all(jnp.broadcast_to(block_map, (16, 2)), PLANE, 0, 0, tiled=T...  17.4 us
    all_gather x1, blocking collectives, shards(): lax.all_gather(coulomb.astype(jnp.bfloat16), 'yh', axis=0, tiled=True)  15.6 us
    all_to_all x1, waiting for transfers between devices, shards(): owned = jnp.sum(lax.all_to_all(plane_sum, 'z', 0, 0, tiled=True), axis=0)  11.1 us
    all_to_all x1, starting transfers between devices, shards(): lax.all_to_all(ordered.reshape(16, 48, 256), PLANE, 0, 0, tiled=True)  9.36 us
    all_to_all x1, waiting for transfers between devices, shards(): lax.all_to_all(ordered.reshape(16, 48, 256), PLANE, 0, 0, tiled=True)  8.08 us
  transfers between devices with their start and end apart: 4, of which 3 were waited for; matrix products, arithmetic and copies ran while one was open for 1% of the time, Pallas kernels for 0%

profile of v2, /device:TPU:1, one launch (start us, length us, event | category | flops | bytes accessed | tf_op | source)
XLA Modules:
  0.0 164.4 jit_solution(7968830093179612117)
XLA Ops:
  0.0 1.4 broadcast_in_dim.63
  1.4 17.4 %all-to-all-start = ((s32[16,1,2]{2,1,0:T(1,128)}), s32[16,1,2]{2,1,0:T(1,128)S(1)}, u32[]{:S(2)}, u32[]{:S(2)}) async-start(s32[16,1,2]{2,1,0:T(1,128)} %broadcast_in_dim.63), calls=%async_computation | async-start | bytes 16384 | tf_op jit(solution)/shard_map/all_to_all | solution.py:100
  18.8 29.6 %all_gather.6 = bf16[32,16,704]{2,1,0:T(8,128)(2,1)S(1)} all-gather(bf16[2,16,704]{2,1,0:T(8,128)(2,1)} %param.7), channel_id=1, replica_groups=mesh['yl'=2,'x'=4,'z'=16,'core'=2,'yh'=4] {'z'}, dimensions={0}, use_global_device_ids=true | all-gather | bytes 765952 | tf_op jit(solution)/shard_map/all_gather | solution.py:103
  48.4 0.2 copy.13
  48.7 0.1 mul.28
  48.9 1.0 fusion.7
  49.9 28.1 %all_to_all.30.picked_ref = bf16[16,64,512]{2,1,0:T(8,128)(2,1)S(1)} all-to-all(bf16[16,64,512]{2,1,0:T(8,128)(2,1)S(1)} %bitcast.31), channel_id=1, replica_groups=mesh['yl'=2,'x'=4,'z'=16,'core'=2,'yh'=4] {'yl','x','core'}, dimensions={0} | all-to-all | bytes 2097152 | tf_op jit(solution)/shard_map/all_to_all | solution.py:111
  78.0 3.0 %block_integrals.1 = f32[16,16,1024]{2,1,0:T(8,128)} custom-call(bf16[16,64,512]{2,1,0:T(8,128)(2,1)S(1)} %all_to_all.30.picked_ref), custom_call_target="tpu_custom_call" | custom-call | flops 268435456 | bytes 2097152 | tf_op jit(solution)/shard_map/block_integrals/pallas_call | solution.py:61
  81.1 5.9 %all-to-all-start.2 = ((f32[4,64,1024]{2,1,0:T(8,128)}), f32[4,64,1024]{2,1,0:T(8,128)S(1)}, u32[]{:S(2)}, u32[]{:S(2)}) async-start(f32[4,64,1024]{2,1,0:T(8,128)} %bitcast.4), calls=%async_computation.2 | async-start | bytes 2097152 | tf_op jit(solution)/shard_map/all_to_all | solution.py:113
  87.0 0.2 reshape.222
  87.2 23.0 %all-to-all-done.2 = f32[4,64,1024]{2,1,0:T(8,128)S(1)} async-done(((f32[4,64,1024]{2,1,0:T(8,128)}), f32[4,64,1024]{2,1,0:T(8,128)S(1)}, u32[]{:S(2)}, u32[]{:S(2)}) %all-to-all-start.2) | async-done | bytes 1048608 | tf_op jit(solution)/shard_map/all_to_all | solution.py:113
  110.3 15.6 %all-gather = bf16[1,256,1024]{2,1,0:T(8,128)(2,1)S(1)} all-gather(bf16[1,64,1024]{2,1,0:T(8,128)(2,1)S(1)} %fusion.19), channel_id=2, replica_groups=mesh['yl'=2,'x'=4,'z'=16,'core'=2,'yh'=4] {'yh'}, dimensions={1}, use_global_device_ids=true | all-gather | bytes 655360 | tf_op jit(solution)/shard_map/all_gather | solution.py:115
  125.9 0.6 fusion.2
  126.5 0.3 copy.14
  126.8 3.2 %fusion.14 = bf16[768,256]{1,0:T(8,128)(2,1)} fusion(f32[256,768]{1,0:T(8,128)S(1)} %fusion.2, bf16[256,1024]{1,0:T(8,128)(2,1)S(1)} %bitcast.33, bf16[1,768,1024]{2,1,0:T(8,128)(2,1)} %param.8, s32[768]{0:T(1024)S(1)} %reshape.222), kind=kOutput, calls=%fused_computation.14 | convolution fusion | flops 705822720 | bytes 3279872 | tf_op jit(solution)/shard_map/dot_general | solution.py:127
  130.0 9.4 %all-to-all-start.3 = ((bf16[16,48,256]{2,1,0:T(8,128)(2,1)}), bf16[16,48,256]{2,1,0:T(8,128)(2,1)S(1)}, u32[]{:S(2)}, u32[]{:S(2)}) async-start(bf16[16,48,256]{2,1,0:T(8,128)(2,1)} %bitcast.11), calls=%async_computation.3 | async-start | bytes 786432 | tf_op jit(solution)/shard_map/all_to_all | solution.py:130
  139.5 0.1 select_reduce_fusion.4
  139.6 0.1 select_reduce_fusion.1
  139.7 8.1 %all-to-all-done.3 = bf16[16,48,256]{2,1,0:T(8,128)(2,1)S(1)} async-done(((bf16[16,48,256]{2,1,0:T(8,128)(2,1)}), bf16[16,48,256]{2,1,0:T(8,128)(2,1)S(1)}, u32[]{:S(2)}, u32[]{:S(2)}) %all-to-all-start.3) | async-done | bytes 393248 | tf_op jit(solution)/shard_map/all_to_all | solution.py:130
  147.9 0.7 all_to_all.23
  148.5 3.6 %all-to-all-start.4 = ((f32[16,1,768]{2,1,0:T(1,128)}), f32[16,1,768]{2,1,0:T(1,128)S(1)}, u32[]{:S(2)}, u32[]{:S(2)}) async-start(f32[16,1,768]{2,1,0:T(1,128)} %all_to_all.23), calls=%async_computation.4 | async-start | bytes 98304 | tf_op jit(solution)/shard_map/all_to_all | solution.py:132
  152.2 0.5 select_reduce_fusion
  152.6 11.1 %all-to-all-done.4 = f32[16,1,768]{2,1,0:T(1,128)S(1)} async-done(((f32[16,1,768]{2,1,0:T(1,128)}), f32[16,1,768]{2,1,0:T(1,128)S(1)}, u32[]{:S(2)}, u32[]{:S(2)}) %all-to-all-start.4) | async-done | bytes 49184 | tf_op jit(solution)/shard_map/all_to_all | solution.py:132
  163.8 0.6 div.44
  (21 shorter events, 0.4 us)
Async XLA Ops:
  0.0 125.9 %copy-start = (bf16[1,768,1024]{2,1,0:T(8,128)(2,1)S(1)}, bf16[1,768,1024]{2,1,0:T(8,128)(2,1)}, u32[]{:S(2)}) copy-start(bf16[1,768,1024]{2,1,0:T(8,128)(2,1)} %param.9) | copy-start | bytes 4718596
  1.4 47.3 %all-to-all-start = ((s32[16,1,2]{2,1,0:T(1,128)}), s32[16,1,2]{2,1,0:T(1,128)S(1)}, u32[]{:S(2)}, u32[]{:S(2)}) async-start(s32[16,1,2]{2,1,0:T(1,128)} %broadcast_in_dim.63), calls=%async_computation | async-start | bytes 16384 | tf_op jit(solution)/shard_map/all_to_all | solution.py:100
  81.1 29.1 %all-to-all-start.2 = ((f32[4,64,1024]{2,1,0:T(8,128)}), f32[4,64,1024]{2,1,0:T(8,128)S(1)}, u32[]{:S(2)}, u32[]{:S(2)}) async-start(f32[4,64,1024]{2,1,0:T(8,128)} %bitcast.4), calls=%async_computation.2 | async-start | bytes 2097152 | tf_op jit(solution)/shard_map/all_to_all | solution.py:113
  126.8 12.7 %copy-start.1 = (s32[768,2]{0,1:T(2,128)S(1)}, s32[768,2]{0,1:T(2,128)}, u32[]{:S(2)}) copy-start(s32[768,2]{0,1:T(2,128)} %param.11) | copy-start | bytes 18436
  126.8 12.7 %copy-start.2 = (f32[16]{0:T(128)S(1)}, f32[16]{0:T(128)}, u32[]{:S(2)}) copy-start(f32[16]{0:T(128)} %param.12) | copy-start | bytes 196
  126.8 12.8 %copy-start.3 = (f32[64]{0:T(128)S(1)}, f32[64]{0:T(128)}, u32[]{:S(2)}) copy-start(f32[64]{0:T(128)} %param.13) | copy-start | bytes 772
  130.0 17.8 %all-to-all-start.3 = ((bf16[16,48,256]{2,1,0:T(8,128)(2,1)}), bf16[16,48,256]{2,1,0:T(8,128)(2,1)S(1)}, u32[]{:S(2)}, u32[]{:S(2)}) async-start(bf16[16,48,256]{2,1,0:T(8,128)(2,1)} %bitcast.11), calls=%async_computation.3 | async-start | bytes 786432 | tf_op jit(solution)/shard_map/all_to_all | solution.py:130
  148.5 15.2 %all-to-all-start.4 = ((f32[16,1,768]{2,1,0:T(1,128)}), f32[16,1,768]{2,1,0:T(1,128)S(1)}, u32[]{:S(2)}, u32[]{:S(2)}) async-start(f32[16,1,768]{2,1,0:T(1,128)} %all_to_all.23), calls=%async_computation.4 | async-start | bytes 98304 | tf_op jit(solution)/shard_map/all_to_all | solution.py:132

commit v3 on v2

--- a/solution.py
+++ b/solution.py
@@ -13,6 +13,8 @@
 PLANE = ("yl", "x", "core")
 GROUP = 4
 LANES = 128
+PAIRS = BLOCK_VIRTUALS**2
+TOP = 14.0
 
 
 def swap_lane_blocks(tiles):
@@ -42,25 +44,31 @@
                 tile = tile.astype(jnp.bfloat16)
                 left_ref[rows, depth] = tile[:BLOCK_VIRTUALS]
                 right_ref[rows, depth] = tile[BLOCK_VIRTUALS:]
-    product_ref[...] = lax.dot_general(
+    product = lax.dot_general(
         left_ref[...],
         right_ref[...],
         (((1,), (1,)), ((), ())),
         preferred_element_type=jnp.float32,
-    ).reshape(product_ref.shape)
+    )
+    largest = jnp.max(jnp.max(jnp.abs(product), axis=0, keepdims=True), axis=1, keepdims=True)
+    power = jnp.ceil(jnp.log2(jnp.maximum(largest, 2.0**-100)))
+    scale = jnp.exp2(TOP - power)
+    product_ref[...] = (product * scale).reshape(product_ref.shape)
+    out_ref[:, :, PAIRS:] = jnp.broadcast_to(power, (AW * AW, LANES)).reshape(AW, AW, LANES)
     for c in range(0, BLOCK_VIRTUALS, GROUP):
         for b in range(0, AW, GROUP):
             lanes = slice(b * BLOCK_VIRTUALS, b * BLOCK_VIRTUALS + LANES)
             tiles = [product_ref[:, c + i, lanes] for i in range(GROUP)]
             for j, tile in enumerate(swap_lane_blocks(tiles)):
-                out_ref[b + j, :, c * BLOCK_VIRTUALS : c * BLOCK_VIRTUALS + LANES] = tile
+                lanes_out = slice(c * BLOCK_VIRTUALS, c * BLOCK_VIRTUALS + LANES)
+                out_ref[b + j, :, lanes_out] = tile
 
 
 def block_integrals(picked):
     side = AW * BLOCK_VIRTUALS
     return pl.pallas_call(
         integrals_kernel,
-        out_shape=jax.ShapeDtypeStruct((AW, AW, BLOCK_VIRTUALS**2), jnp.float32),
+        out_shape=jax.ShapeDtypeStruct((AW, AW, PAIRS + LANES), jnp.float32),
         in_specs=[pl.BlockSpec(memory_space=pltpu.VMEM)],
         out_specs=pl.BlockSpec(memory_space=pltpu.VMEM),
         scratch_shapes=[
@@ -109,9 +117,11 @@
     picked = select_rows(one_hot_rows(wanted, NV), line)
     picked = picked.reshape(16, 2 * BLOCK_VIRTUALS, AW * q_line)
     picked = lax.all_to_all(picked, PLANE, 0, 0, tiled=True)
-    partial_sum = block_integrals(picked).reshape(4, 4 * AW, -1)
+    partial_sum = block_integrals(picked).astype(jnp.float16).reshape(4, 4 * AW, -1)
     quarters = lax.all_to_all(partial_sum, "yh", 0, 0, tiled=True)
-    coulomb = quarters[0] + quarters[1] + quarters[2] + quarters[3]
+    quarters = quarters.astype(jnp.float32)
+    unscale = jnp.exp2(quarters[:, :1, PAIRS : PAIRS + 1] - TOP)
+    coulomb = jnp.sum(quarters[:, :, :PAIRS] * unscale, axis=0)
     mirrored = lax.all_gather(coulomb.astype(jnp.bfloat16), "yh", axis=0, tiled=True)
     weights = mirrored.reshape(AW, AW, -1).transpose(1, 0, 2).reshape(AW * AW, -1)
     direct_term = lax.dot_general(

time: 165 us -> 157 us (0.952)
  waiting for transfers between devices: 42.2 us -> 32.7 us
  starting transfers between devices: 36.3 us -> 39.3 us
  blocking collectives: 73.2 us -> 71.3 us
    all_to_all x1, waiting for transfers between devices: 23 us -> 13.6 us  [shards(): quarters = lax.all_to_all(partial_sum, 'yh', 0, 0, tiled=True)]
    all_to_all x1, starting transfers between devices: 9.36 us -> 12.4 us  [shards(): lax.all_to_all(ordered.reshape(16, 48, 256), PLANE, 0, 0, tiled=True)]
    all_gather x1, blocking collectives: 15.6 us -> 13.6 us  [shards(): lax.all_gather(coulomb.astype(jnp.bfloat16), 'yh', axis=0, tiled=True)]
where the time goes in v3:
time: 157 us; the launch traced here: 156 us
  blocking collectives  71.3 us (45%)
  starting transfers between devices  39.3 us (25%)
  waiting for transfers between devices  32.7 us (21%)
  matrix products  4.88 us (3%)
  local copies, waits for them, and re-layouts  3.56 us (2%)
  Pallas kernels  2.26 us (1%)
  other arithmetic  2.16 us (1%)
    all_gather x1, blocking collectives, shards(): line = lax.all_gather(factor, 'z', axis=0, tiled=True)  29.6 us
    all_to_all x1, blocking collectives, shards(): picked = lax.all_to_all(picked, PLANE, 0, 0, tiled=True)  28.1 us
    all_to_all x1, starting transfers between devices, shards(): lax.all_to_all(jnp.broadcast_to(block_map, (16, 2)), PLANE, 0, 0, tiled=T...  17.4 us
    all_gather x1, blocking collectives, shards(): lax.all_gather(coulomb.astype(jnp.bfloat16), 'yh', axis=0, tiled=True)  13.6 us
    all_to_all x1, waiting for transfers between devices, shards(): quarters = lax.all_to_all(partial_sum, 'yh', 0, 0, tiled=True)  13.6 us
    all_to_all x1, starting transfers between devices, shards(): lax.all_to_all(ordered.reshape(16, 48, 256), PLANE, 0, 0, tiled=True)  12.4 us
    all_to_all x1, waiting for transfers between devices, shards(): owned = jnp.sum(lax.all_to_all(plane_sum, 'z', 0, 0, tiled=True), axis=0)  11 us
    all_to_all x1, waiting for transfers between devices, shards(): lax.all_to_all(ordered.reshape(16, 48, 256), PLANE, 0, 0, tiled=True)  8.08 us
  transfers between devices with their start and end apart: 4, of which 3 were waited for; matrix products, arithmetic and copies ran while one was open for 1% of the time, Pallas kernels for 0%

profile of v3, /device:TPU:1, one launch (start us, length us, event | category | flops | bytes accessed | tf_op | source)
XLA Modules:
  0.0 156.3 jit_solution(17975718818441233908)
XLA Ops:
  0.0 1.4 broadcast_in_dim.63
  1.4 17.4 %all-to-all-start = ((s32[16,1,2]{2,1,0:T(1,128)}), s32[16,1,2]{2,1,0:T(1,128)S(1)}, u32[]{:S(2)}, u32[]{:S(2)}) async-start(s32[16,1,2]{2,1,0:T(1,128)} %broadcast_in_dim.63), calls=%async_computation | async-start | bytes 16384 | tf_op jit(solution)/shard_map/all_to_all | solution.py:108
  18.8 29.6 %all_gather.6 = bf16[32,16,704]{2,1,0:T(8,128)(2,1)S(1)} all-gather(bf16[2,16,704]{2,1,0:T(8,128)(2,1)} %param.7), channel_id=1, replica_groups=mesh['yl'=2,'x'=4,'z'=16,'core'=2,'yh'=4] {'z'}, dimensions={0}, use_global_device_ids=true | all-gather | bytes 765952 | tf_op jit(solution)/shard_map/all_gather | solution.py:111
  48.4 0.2 copy.18
  48.9 1.0 fusion.7
  49.9 28.1 %all_to_all.30.picked_ref = bf16[16,64,512]{2,1,0:T(8,128)(2,1)S(1)} all-to-all(bf16[16,64,512]{2,1,0:T(8,128)(2,1)S(1)} %bitcast.29), channel_id=1, replica_groups=mesh['yl'=2,'x'=4,'z'=16,'core'=2,'yh'=4] {'yl','x','core'}, dimensions={0} | all-to-all | bytes 2097152 | tf_op jit(solution)/shard_map/all_to_all | solution.py:119
  78.0 2.3 %block_integrals.1 = f32[16,16,1152]{2,1,0:T(8,128)S(1)} custom-call(bf16[16,64,512]{2,1,0:T(8,128)(2,1)S(1)} %all_to_all.30.picked_ref), custom_call_target="tpu_custom_call" | custom-call | flops 268435456 | bytes 2097152 | tf_op jit(solution)/shard_map/block_integrals/pallas_call | solution.py:69
  80.3 0.9 convert_element_type.25
  81.2 5.9 %all-to-all-start.2 = ((f16[4,64,1152]{2,1,0:T(8,128)(2,1)}), f16[4,64,1152]{2,1,0:T(8,128)(2,1)S(1)}, u32[]{:S(2)}, u32[]{:S(2)}) async-start(f16[4,64,1152]{2,1,0:T(8,128)(2,1)} %bitcast.4), calls=%async_computation.2 | async-start | bytes 1179648 | tf_op jit(solution)/shard_map/all_to_all | solution.py:121
  87.1 0.2 reshape.218
  87.3 13.6 %all-to-all-done.2 = f16[4,64,1152]{2,1,0:T(8,128)(2,1)S(1)} async-done(((f16[4,64,1152]{2,1,0:T(8,128)(2,1)}), f16[4,64,1152]{2,1,0:T(8,128)(2,1)S(1)}, u32[]{:S(2)}, u32[]{:S(2)}) %all-to-all-start.2) | async-done | bytes 589856 | tf_op jit(solution)/shard_map/all_to_all | solution.py:121
  101.1 0.1 fusion.18
  101.3 13.6 %all_gather.7 = bf16[256,1024]{1,0:T(8,128)(2,1)S(1)} all-gather(bf16[64,1024]{1,0:T(8,128)(2,1)S(1)} %fusion.18), channel_id=1, replica_groups=mesh['yl'=2,'x'=4,'z'=16,'core'=2,'yh'=4] {'yh'}, dimensions={0}, use_global_device_ids=true | all-gather | bytes 655360 | tf_op jit(solution)/shard_map/all_gather | solution.py:125
  114.9 0.6 fusion.2
  115.5 0.3 copy.19
  115.8 3.2 %fusion.14 = bf16[768,256]{1,0:T(8,128)(2,1)} fusion(f32[256,768]{1,0:T(8,128)S(1)} %fusion.2, bf16[256,1024]{1,0:T(8,128)(2,1)S(1)} %bitcast.31, bf16[1,768,1024]{2,1,0:T(8,128)(2,1)} %param.8, s32[768]{0:T(1024)S(1)} %reshape.218), kind=kOutput, calls=%fused_computation.14 | convolution fusion | flops 705822720 | bytes 3279872 | tf_op jit(solution)/shard_map/dot_general | solution.py:137
  119.1 12.4 %all-to-all-start.3 = ((bf16[16,48,256]{2,1,0:T(8,128)(2,1)}), bf16[16,48,256]{2,1,0:T(8,128)(2,1)S(1)}, u32[]{:S(2)}, u32[]{:S(2)}) async-start(bf16[16,48,256]{2,1,0:T(8,128)(2,1)} %bitcast.10), calls=%async_computation.3 | async-start | bytes 786432 | tf_op jit(solution)/shard_map/all_to_all | solution.py:140
  131.7 0.1 select_reduce_fusion.1
  131.8 8.1 %all-to-all-done.3 = bf16[16,48,256]{2,1,0:T(8,128)(2,1)S(1)} async-done(((bf16[16,48,256]{2,1,0:T(8,128)(2,1)}), bf16[16,48,256]{2,1,0:T(8,128)(2,1)S(1)}, u32[]{:S(2)}, u32[]{:S(2)}) %all-to-all-start.3) | async-done | bytes 393248 | tf_op jit(solution)/shard_map/all_to_all | solution.py:140
  140.0 0.7 all_to_all.23
  140.6 3.5 %all-to-all-start.4 = ((f32[16,1,768]{2,1,0:T(1,128)}), f32[16,1,768]{2,1,0:T(1,128)S(1)}, u32[]{:S(2)}, u32[]{:S(2)}) async-start(f32[16,1,768]{2,1,0:T(1,128)} %all_to_all.23), calls=%async_computation.4 | async-start | bytes 98304 | tf_op jit(solution)/shard_map/all_to_all | solution.py:142
  144.2 0.5 select_reduce_fusion
  144.6 11.0 %all-to-all-done.4 = f32[16,1,768]{2,1,0:T(1,128)S(1)} async-done(((f32[16,1,768]{2,1,0:T(1,128)}), f32[16,1,768]{2,1,0:T(1,128)S(1)}, u32[]{:S(2)}, u32[]{:S(2)}) %all-to-all-start.4) | async-done | bytes 49184 | tf_op jit(solution)/shard_map/all_to_all | solution.py:142
  155.7 0.6 div.44
  (24 shorter events, 0.8 us)
Async XLA Ops:
  0.0 114.9 %copy-start = (bf16[1,768,1024]{2,1,0:T(8,128)(2,1)S(1)}, bf16[1,768,1024]{2,1,0:T(8,128)(2,1)}, u32[]{:S(2)}) copy-start(bf16[1,768,1024]{2,1,0:T(8,128)(2,1)} %param.9) | copy-start | bytes 4718596
  1.4 47.3 %all-to-all-start = ((s32[16,1,2]{2,1,0:T(1,128)}), s32[16,1,2]{2,1,0:T(1,128)S(1)}, u32[]{:S(2)}, u32[]{:S(2)}) async-start(s32[16,1,2]{2,1,0:T(1,128)} %broadcast_in_dim.63), calls=%async_computation | async-start | bytes 16384 | tf_op jit(solution)/shard_map/all_to_all | solution.py:108
  81.2 19.7 %all-to-all-start.2 = ((f16[4,64,1152]{2,1,0:T(8,128)(2,1)}), f16[4,64,1152]{2,1,0:T(8,128)(2,1)S(1)}, u32[]{:S(2)}, u32[]{:S(2)}) async-start(f16[4,64,1152]{2,1,0:T(8,128)(2,1)} %bitcast.4), calls=%async_computation.2 | async-start | bytes 1179648 | tf_op jit(solution)/shard_map/all_to_all | solution.py:121
  115.8 15.7 %copy-start.1 = (s32[768,2]{0,1:T(2,128)S(1)}, s32[768,2]{0,1:T(2,128)}, u32[]{:S(2)}) copy-start(s32[768,2]{0,1:T(2,128)} %param.11) | copy-start | bytes 18436
  115.8 15.8 %copy-start.2 = (f32[16]{0:T(128)S(1)}, f32[16]{0:T(128)}, u32[]{:S(2)}) copy-start(f32[16]{0:T(128)} %param.12) | copy-start | bytes 196
  115.8 15.9 %copy-start.3 = (f32[64]{0:T(128)S(1)}, f32[64]{0:T(128)}, u32[]{:S(2)}) copy-start(f32[64]{0:T(128)} %param.13) | copy-start | bytes 772
  119.1 20.8 %all-to-all-start.3 = ((bf16[16,48,256]{2,1,0:T(8,128)(2,1)}), bf16[16,48,256]{2,1,0:T(8,128)(2,1)S(1)}, u32[]{:S(2)}, u32[]{:S(2)}) async-start(bf16[16,48,256]{2,1,0:T(8,128)(2,1)} %bitcast.10), calls=%async_computation.3 | async-start | bytes 786432 | tf_op jit(solution)/shard_map/all_to_all | solution.py:140
  140.6 15.0 %all-to-all-start.4 = ((f32[16,1,768]{2,1,0:T(1,128)}), f32[16,1,768]{2,1,0:T(1,128)S(1)}, u32[]{:S(2)}, u32[]{:S(2)}) async-start(f32[16,1,768]{2,1,0:T(1,128)} %all_to_all.23), calls=%async_computation.4 | async-start | bytes 98304 | tf_op jit(solution)/shard_map/all_to_all | solution.py:142

commit v4 on v3

--- a/solution.py
+++ b/solution.py
@@ -64,6 +64,51 @@
                 out_ref[b + j, :, lanes_out] = tile
 
 
+def select_matmul(hot, rows):
+    return jnp.dot(hot, rows, preferred_element_type=jnp.float32).astype(jnp.bfloat16)
+
+
+def residual_kernel(forward_ref, reversed_ref, mirrored_ref, out_ref):
+    cells = AW * AW
+    row = lax.broadcasted_iota(jnp.int32, (cells, cells), 0)
+    col = lax.broadcasted_iota(jnp.int32, (cells, cells), 1)
+    other = lax.bitwise_and(row, AW - 1) * AW + lax.shift_right_logical(row, 4)
+    weights = select_matmul((col == other).astype(jnp.bfloat16), mirrored_ref[...])
+    across = (((1,), (1,)), ((), ()))
+    piece = 96
+    row = lax.broadcasted_iota(jnp.int32, (piece, piece), 0)
+    col = lax.broadcasted_iota(jnp.int32, (piece, piece), 1)
+    core = (row >= piece // 2).astype(jnp.int32)
+    within = row - core * (piece // 2)
+    line = lax.shift_right_logical(within * 171, 9)
+    hot = (col == line * 3 + within + core * 3).astype(jnp.bfloat16)
+    for start in range(0, 768, piece):
+        rows = slice(start, start + piece)
+        term = lax.dot_general(
+            forward_ref[0, rows], weights, across, preferred_element_type=jnp.float32
+        ) + lax.dot_general(
+            reversed_ref[0, rows], mirrored_ref[...], across, preferred_element_type=jnp.float32
+        )
+        ordered = select_matmul(hot, term.astype(jnp.bfloat16))
+        at = start // (piece // 2)
+        out_ref[at] = ordered[: piece // 2]
+        out_ref[at + 1] = ordered[piece // 2 :]
+
+
+def residual_terms(forward, backward, mirrored):
+    return pl.pallas_call(
+        residual_kernel,
+        out_shape=jax.ShapeDtypeStruct((16, 48, AW * AW), jnp.bfloat16),
+        in_specs=[pl.BlockSpec(memory_space=pltpu.VMEM)] * 3,
+        out_specs=pl.BlockSpec(memory_space=pltpu.VMEM),
+        compiler_params=pltpu.CompilerParams(vmem_limit_bytes=24 * 1024 * 1024),
+        cost_estimate=pl.CostEstimate(
+            flops=4 * 768 * 256 * 1024, bytes_accessed=4 * 1024 * 1024, transcendentals=0
+        ),
+        name="residual_terms",
+    )(forward, backward, mirrored)
+
+
 def block_integrals(picked):
     side = AW * BLOCK_VIRTUALS
     return pl.pallas_call(
@@ -123,25 +168,12 @@
     unscale = jnp.exp2(quarters[:, :1, PAIRS : PAIRS + 1] - TOP)
     coulomb = jnp.sum(quarters[:, :, :PAIRS] * unscale, axis=0)
     mirrored = lax.all_gather(coulomb.astype(jnp.bfloat16), "yh", axis=0, tiled=True)
-    weights = mirrored.reshape(AW, AW, -1).transpose(1, 0, 2).reshape(AW * AW, -1)
-    direct_term = lax.dot_general(
-        amplitude_forward[0], weights, (((1,), (1,)), ((), ())), preferred_element_type=jnp.float32
-    )
-    swapped = lax.dot_general(
-        amplitude_reversed[0], mirrored, (((1,), (1,)), ((), ())), preferred_element_type=jnp.float32
-    )
-    slot_term = (direct_term + swapped).astype(jnp.bfloat16)
-    row = jnp.arange(768, dtype=jnp.int32)
-    source = jnp.arange(768, dtype=jnp.int32).reshape(8, 16, 2, 3).transpose(0, 2, 1, 3).reshape(-1)
-    hot = one_hot_rows(source, 768)
-    ordered = lax.dot_general(
-        hot, slot_term, (((1,), (0,)), ((), ())), preferred_element_type=jnp.float32
-    ).astype(jnp.bfloat16)
-    ordered = lax.all_to_all(ordered.reshape(16, 48, 256), PLANE, 0, 0, tiled=True)
-    plane_sum = jnp.sum(ordered.astype(jnp.float32), axis=0).reshape(16, 768)
+    ordered = residual_terms(amplitude_forward, amplitude_reversed, mirrored)
+    ordered = lax.all_to_all(ordered, PLANE, 0, 0, tiled=True)
+    plane_sum = jnp.sum(ordered.astype(jnp.float32), axis=0).reshape(16, 1, 768)
     owned = jnp.sum(lax.all_to_all(plane_sum, "z", 0, 0, tiled=True), axis=0)
 
-    owned_len = owned.shape[0]
+    owned_len = owned.shape[1]
     offset = lax.axis_index(BLK) * owned_len
     flat_index = offset + jnp.arange(owned_len, dtype=jnp.int32)
     pair_at = flat_index // (AW * AW)
@@ -153,7 +185,7 @@
     energy_a = table_lookup(cell_index // AW, virt_energy)
     energy_b = table_lookup(cell_index % AW, virt_energy)
     denominator = owned_pair - energy_a - energy_b
-    return (owned / denominator).reshape(1, owned_len)
+    return owned / denominator.reshape(1, owned_len)
 
 
 def solution(mesh):

time: 157 us -> 157 us (level)
  blocking collectives: 71.3 us -> 92.1 us
  waiting for transfers between devices: 32.7 us -> 19.1 us
  starting transfers between devices: 39.3 us -> 31.7 us
  Pallas kernels: 2.26 us -> 8.25 us
  matrix products: 4.88 us -> 1.04 us
    all_to_all x0 -> x1, blocking collectives: none -> 20 us  [shards(): quarters = lax.all_to_all(partial_sum, 'yh', 0, 0, tiled=True)]
    all_to_all x2 -> x1, waiting for transfers between devices: 21.7 us -> 8.16 us  [shards(): ordered = lax.all_to_all(ordered, PLANE, 0, 0, tiled=True)]
    all_to_all x2 -> x1, starting transfers between devices: 18.4 us -> 10.8 us  [shards(): ordered = lax.all_to_all(ordered, PLANE, 0, 0, tiled=True)]
    pallas_call x0 -> x1, Pallas kernels: none -> 5.98 us  [residual_terms(): pl.pallas_call(residual_kernel, out_shape=jax.ShapeDtypeStruct((16, 48, A...]
    dot_general x2 -> x0, matrix products: 3.85 us -> none  [the longest x1 3.24 us: shards(): lax.dot_general(hot, slot_term, (((1,), (0,)), ((), ())), preferred_eleme...]
  transfers between devices with their start and end apart: 4 -> 3, of which waited for: 3 -> 2; matrix products, arithmetic and copies ran while one was open for 1% -> 1% of each run, Pallas kernels for 0% -> 0%
where the time goes in v4:
time: 157 us
  blocking collectives  92.1 us (59%)
  starting transfers between devices  31.7 us (20%)
  waiting for transfers between devices  19.1 us (12%)
  Pallas kernels  8.25 us (5%)
  local copies, waits for them, and re-layouts  2.94 us (2%)
    all_gather x1, blocking collectives, shards(): line = lax.all_gather(factor, 'z', axis=0, tiled=True)  29.6 us
    all_to_all x1, blocking collectives, shards(): picked = lax.all_to_all(picked, PLANE, 0, 0, tiled=True)  28.1 us
    all_to_all x1, blocking collectives, shards(): quarters = lax.all_to_all(partial_sum, 'yh', 0, 0, tiled=True)  20 us
    all_to_all x1, starting transfers between devices, shards(): lax.all_to_all(jnp.broadcast_to(block_map, (16, 2)), PLANE, 0, 0, tiled=T...  17.4 us
    all_gather x1, blocking collectives, shards(): lax.all_gather(coulomb.astype(jnp.bfloat16), 'yh', axis=0, tiled=True)  14.4 us
    all_to_all x1, waiting for transfers between devices, shards(): owned = jnp.sum(lax.all_to_all(plane_sum, 'z', 0, 0, tiled=True), axis=0)  11 us
    all_to_all x1, starting transfers between devices, shards(): ordered = lax.all_to_all(ordered, PLANE, 0, 0, tiled=True)  10.8 us
    all_to_all x1, waiting for transfers between devices, shards(): ordered = lax.all_to_all(ordered, PLANE, 0, 0, tiled=True)  8.16 us
  transfers between devices with their start and end apart: 3, of which 2 were waited for; matrix products, arithmetic and copies ran while one was open for 1% of the time, Pallas kernels for 0%

profile of v4, /device:TPU:1, one launch (start us, length us, event | category | flops | bytes accessed | tf_op | source)
XLA Modules:
  0.0 156.7 jit_solution(1459492754400614674)
XLA Ops:
  0.0 1.3 broadcast_in_dim.63
  1.3 17.4 %all-to-all-start = ((s32[16,1,2]{2,1,0:T(1,128)}), s32[16,1,2]{2,1,0:T(1,128)S(1)}, u32[]{:S(2)}, u32[]{:S(2)}) async-start(s32[16,1,2]{2,1,0:T(1,128)} %broadcast_in_dim.63), calls=%async_computation | async-start | bytes 16384 | tf_op jit(solution)/shard_map/all_to_all | solution.py:153
  18.7 29.6 %all_gather.6 = bf16[32,16,704]{2,1,0:T(8,128)(2,1)S(1)} all-gather(bf16[2,16,704]{2,1,0:T(8,128)(2,1)} %param.7), channel_id=1, replica_groups=mesh['yl'=2,'x'=4,'z'=16,'core'=2,'yh'=4] {'z'}, dimensions={0}, use_global_device_ids=true | all-gather | bytes 765952 | tf_op jit(solution)/shard_map/all_gather | solution.py:156
  48.3 0.2 copy.13
  48.5 0.1 mul.38
  48.7 0.1 add.87
  48.8 1.0 fusion.2
  49.8 28.1 %all_to_all.26.picked_ref = bf16[16,64,512]{2,1,0:T(8,128)(2,1)S(1)} all-to-all(bf16[16,64,512]{2,1,0:T(8,128)(2,1)S(1)} %bitcast.8), channel_id=1, replica_groups=mesh['yl'=2,'x'=4,'z'=16,'core'=2,'yh'=4] {'yl','x','core'}, dimensions={0} | all-to-all | bytes 2097152 | tf_op jit(solution)/shard_map/all_to_all | solution.py:164
  77.9 2.3 %block_integrals.1 = f32[16,16,1152]{2,1,0:T(8,128)S(1)} custom-call(bf16[16,64,512]{2,1,0:T(8,128)(2,1)S(1)} %all_to_all.26.picked_ref), custom_call_target="tpu_custom_call" | custom-call | flops 268435456 | bytes 2097152 | tf_op jit(solution)/shard_map/block_integrals/pallas_call | solution.py:114
  80.2 20.0 %all_to_all.27 = f16[4,64,1152]{2,1,0:T(8,128)(2,1)S(1)} all-to-all(f16[4,64,1152]{2,1,0:T(8,128)(2,1)S(1)} %bitcast.7), channel_id=1, replica_groups=mesh['yl'=2,'x'=4,'z'=16,'core'=2,'yh'=4] {'yh'}, dimensions={0} | all-to-all | bytes 1179648 | tf_op jit(solution)/shard_map/all_to_all | solution.py:166
  100.3 0.1 convert_element_type.18
  100.4 0.1 fusion.13
  100.5 0.1 fusion.3
  100.7 14.4 %all_gather.7.mirrored_ref = bf16[256,1024]{1,0:T(8,128)(2,1)S(1)} all-gather(bf16[64,1024]{1,0:T(8,128)(2,1)S(1)} %fusion.3), channel_id=1, replica_groups=mesh['yl'=2,'x'=4,'z'=16,'core'=2,'yh'=4] {'yh'}, dimensions={0}, use_global_device_ids=true | all-gather | bytes 655360 | tf_op jit(solution)/shard_map/all_gather | solution.py:170
  115.1 6.0 %residual_terms.1 = bf16[16,48,256]{2,1,0:T(8,128)(2,1)} custom-call(bf16[1,768,1024]{2,1,0:T(8,128)(2,1)S(1)} %copy-done, bf16[1,768,1024]{2,1,0:T(8,128)(2,1)S(1)} %copy-done.1, bf16[256,1024]{1,0:T(8,128)(2,1)S(1)} %all_gather.7.mirrored_ref), custom_call_target="tpu_custom_call" | custom-call | flops 805306368 | bytes 4194304 | tf_op jit(solution)/shard_map/residual_terms/pallas_call | solution.py:99
  121.1 10.8 %all-to-all-start.3 = ((bf16[16,48,256]{2,1,0:T(8,128)(2,1)}), bf16[16,48,256]{2,1,0:T(8,128)(2,1)S(1)}, u32[]{:S(2)}, u32[]{:S(2)}) async-start(bf16[16,48,256]{2,1,0:T(8,128)(2,1)} %residual_terms.1), calls=%async_computation.3 | async-start | bytes 786432 | tf_op jit(solution)/shard_map/all_to_all | solution.py:172
  131.9 0.1 select_reduce_fusion.4
  132.0 0.1 select_reduce_fusion.1
  132.2 8.2 %all-to-all-done.3 = bf16[16,48,256]{2,1,0:T(8,128)(2,1)S(1)} async-done(((bf16[16,48,256]{2,1,0:T(8,128)(2,1)}), bf16[16,48,256]{2,1,0:T(8,128)(2,1)S(1)}, u32[]{:S(2)}, u32[]{:S(2)}) %all-to-all-start.3) | async-done | bytes 393248 | tf_op jit(solution)/shard_map/all_to_all | solution.py:172
  140.4 0.7 reshape.144
  141.1 3.5 %all-to-all-start.4 = ((f32[16,1,768]{2,1,0:T(1,128)}), f32[16,1,768]{2,1,0:T(1,128)S(1)}, u32[]{:S(2)}, u32[]{:S(2)}) async-start(f32[16,1,768]{2,1,0:T(1,128)} %reshape.144), calls=%async_computation.4 | async-start | bytes 98304 | tf_op jit(solution)/shard_map/all_to_all | solution.py:174
  144.6 0.5 select_reduce_fusion
  145.1 11.0 %all-to-all-done.4 = f32[16,1,768]{2,1,0:T(1,128)S(1)} async-done(((f32[16,1,768]{2,1,0:T(1,128)}), f32[16,1,768]{2,1,0:T(1,128)S(1)}, u32[]{:S(2)}, u32[]{:S(2)}) %all-to-all-start.4) | async-done | bytes 49184 | tf_op jit(solution)/shard_map/all_to_all | solution.py:174
  156.1 0.6 div.45
  (21 shorter events, 0.4 us)
Async XLA Ops:
  1.3 47.3 %all-to-all-start = ((s32[16,1,2]{2,1,0:T(1,128)}), s32[16,1,2]{2,1,0:T(1,128)S(1)}, u32[]{:S(2)}, u32[]{:S(2)}) async-start(s32[16,1,2]{2,1,0:T(1,128)} %broadcast_in_dim.63), calls=%async_computation | async-start | bytes 16384 | tf_op jit(solution)/shard_map/all_to_all | solution.py:153
  100.3 14.8 %copy-start = (bf16[1,768,1024]{2,1,0:T(8,128)(2,1)S(1)}, bf16[1,768,1024]{2,1,0:T(8,128)(2,1)}, u32[]{:S(2)}) copy-start(bf16[1,768,1024]{2,1,0:T(8,128)(2,1)} %forward_ref.1) | copy-start | bytes 4718596
  100.3 14.8 %copy-start.1 = (bf16[1,768,1024]{2,1,0:T(8,128)(2,1)S(1)}, bf16[1,768,1024]{2,1,0:T(8,128)(2,1)}, u32[]{:S(2)}) copy-start(bf16[1,768,1024]{2,1,0:T(8,128)(2,1)} %reversed_ref.1) | copy-start | bytes 4718596
  115.1 16.8 %copy-start.2 = (s32[768,2]{0,1:T(2,128)S(1)}, s32[768,2]{0,1:T(2,128)}, u32[]{:S(2)}) copy-start(s32[768,2]{0,1:T(2,128)} %param.11) | copy-start | bytes 18436
  115.1 16.8 %copy-start.3 = (f32[16]{0:T(128)S(1)}, f32[16]{0:T(128)}, u32[]{:S(2)}) copy-start(f32[16]{0:T(128)} %param.12) | copy-start | bytes 196
  115.1 16.9 %copy-start.4 = (f32[64]{0:T(128)S(1)}, f32[64]{0:T(128)}, u32[]{:S(2)}) copy-start(f32[64]{0:T(128)} %param.13) | copy-start | bytes 772
  121.1 19.2 %all-to-all-start.3 = ((bf16[16,48,256]{2,1,0:T(8,128)(2,1)}), bf16[16,48,256]{2,1,0:T(8,128)(2,1)S(1)}, u32[]{:S(2)}, u32[]{:S(2)}) async-start(bf16[16,48,256]{2,1,0:T(8,128)(2,1)} %residual_terms.1), calls=%async_computation.3 | async-start | bytes 786432 | tf_op jit(solution)/shard_map/all_to_all | solution.py:172
  141.1 15.0 %all-to-all-start.4 = ((f32[16,1,768]{2,1,0:T(1,128)}), f32[16,1,768]{2,1,0:T(1,128)S(1)}, u32[]{:S(2)}, u32[]{:S(2)}) async-start(f32[16,1,768]{2,1,0:T(1,128)} %reshape.144), calls=%async_computation.4 | async-start | bytes 98304 | tf_op jit(solution)/shard_map/all_to_all | solution.py:174

commit v5 on v4

--- a/solution.py
+++ b/solution.py
@@ -68,13 +68,22 @@
     return jnp.dot(hot, rows, preferred_element_type=jnp.float32).astype(jnp.bfloat16)
 
 
-def residual_kernel(forward_ref, reversed_ref, mirrored_ref, out_ref):
+def residual_kernel(forward_ref, reversed_ref, mirrored_ref, out_ref, term_ref):
     cells = AW * AW
     row = lax.broadcasted_iota(jnp.int32, (cells, cells), 0)
     col = lax.broadcasted_iota(jnp.int32, (cells, cells), 1)
     other = lax.bitwise_and(row, AW - 1) * AW + lax.shift_right_logical(row, 4)
-    weights = select_matmul((col == other).astype(jnp.bfloat16), mirrored_ref[...])
+    hot = (col == other).astype(jnp.bfloat16)
+    weights = select_matmul(hot, mirrored_ref[...])
     across = (((1,), (1,)), ((), ()))
+    term_ref[...] = (
+        lax.dot_general(
+            forward_ref[0], weights, across, preferred_element_type=jnp.float32
+        )
+        + lax.dot_general(
+            reversed_ref[0], mirrored_ref[...], across, preferred_element_type=jnp.float32
+        )
+    ).astype(jnp.bfloat16)
     piece = 96
     row = lax.broadcasted_iota(jnp.int32, (piece, piece), 0)
     col = lax.broadcasted_iota(jnp.int32, (piece, piece), 1)
@@ -82,25 +91,20 @@
     within = row - core * (piece // 2)
     line = lax.shift_right_logical(within * 171, 9)
     hot = (col == line * 3 + within + core * 3).astype(jnp.bfloat16)
-    for start in range(0, 768, piece):
-        rows = slice(start, start + piece)
-        term = lax.dot_general(
-            forward_ref[0, rows], weights, across, preferred_element_type=jnp.float32
-        ) + lax.dot_general(
-            reversed_ref[0, rows], mirrored_ref[...], across, preferred_element_type=jnp.float32
-        )
-        ordered = select_matmul(hot, term.astype(jnp.bfloat16))
-        at = start // (piece // 2)
-        out_ref[at] = ordered[: piece // 2]
-        out_ref[at + 1] = ordered[piece // 2 :]
+    for at in range(8):
+        ordered = select_matmul(hot, term_ref[at * piece : (at + 1) * piece])
+        rows = slice(at // 4 * (piece // 2), (at // 4 + 1) * (piece // 2))
+        out_ref[at % 4 * 2, rows] = ordered[: piece // 2]
+        out_ref[at % 4 * 2 + 1, rows] = ordered[piece // 2 :]
 
 
 def residual_terms(forward, backward, mirrored):
     return pl.pallas_call(
         residual_kernel,
-        out_shape=jax.ShapeDtypeStruct((16, 48, AW * AW), jnp.bfloat16),
+        out_shape=jax.ShapeDtypeStruct((8, 96, AW * AW), jnp.bfloat16),
         in_specs=[pl.BlockSpec(memory_space=pltpu.VMEM)] * 3,
         out_specs=pl.BlockSpec(memory_space=pltpu.VMEM),
+        scratch_shapes=[pltpu.VMEM((768, AW * AW), jnp.bfloat16)],
         compiler_params=pltpu.CompilerParams(vmem_limit_bytes=24 * 1024 * 1024),
         cost_estimate=pl.CostEstimate(
             flops=4 * 768 * 256 * 1024, bytes_accessed=4 * 1024 * 1024, transcendentals=0
@@ -169,9 +173,9 @@
     coulomb = jnp.sum(quarters[:, :, :PAIRS] * unscale, axis=0)
     mirrored = lax.all_gather(coulomb.astype(jnp.bfloat16), "yh", axis=0, tiled=True)
     ordered = residual_terms(amplitude_forward, amplitude_reversed, mirrored)
-    ordered = lax.all_to_all(ordered, PLANE, 0, 0, tiled=True)
-    plane_sum = jnp.sum(ordered.astype(jnp.float32), axis=0).reshape(16, 1, 768)
-    owned = jnp.sum(lax.all_to_all(plane_sum, "z", 0, 0, tiled=True), axis=0)
+    ordered = lax.all_to_all(ordered, ("x", "core"), 0, 0, tiled=True)
+    near_sum = jnp.sum(ordered.astype(jnp.float32), axis=0).reshape(32, 1, 768)
+    owned = jnp.sum(lax.all_to_all(near_sum, ("yl", "z"), 0, 0, tiled=True), axis=0)
 
     owned_len = owned.shape[1]
     offset = lax.axis_index(BLK) * owned_len

time: 157 us -> 158 us (level)
  blocking collectives: 92.1 us -> 71.3 us
  waiting for transfers between devices: 19.1 us -> 34.8 us
  starting transfers between devices: 31.7 us -> 39.4 us
  Pallas kernels: 8.25 us -> 4.37 us
  other arithmetic: 1.34 us -> 3.25 us
    all_to_all x1 -> x0, blocking collectives: 20 us -> none  [shards(): quarters = lax.all_to_all(partial_sum, 'yh', 0, 0, tiled=True)]
    all_to_all x2 -> x3, waiting for transfers between devices: 19.1 us -> 34.8 us  [the longest x1 13.9 us: shards(): quarters = lax.all_to_all(partial_sum, 'yh', 0, 0, tiled=True)]
    all_to_all x2 -> x3, starting transfers between devices: 14.2 us -> 22 us  [the longest x1 10.1 us: shards(): ordered = lax.all_to_all(ordered, ('x', 'core'), 0, 0, tiled=True)]
    pallas_call x1, Pallas kernels: 5.98 us -> 2.11 us  [residual_terms(): pl.pallas_call(residual_kernel, out_shape=jax.ShapeDtypeStruct((8, 96, AW...]
  transfers between devices with their start and end apart: 3 -> 4, of which waited for: 2 -> 3; matrix products, arithmetic and copies ran while one was open for 1% -> 1% of each run, Pallas kernels for 0% -> 0%
where the time goes in v5:
time: 158 us; the launch traced here: 157 us
  blocking collectives  71.3 us (45%)
  starting transfers between devices  39.4 us (25%)
  waiting for transfers between devices  34.8 us (22%)
  Pallas kernels  4.37 us (3%)
  other arithmetic  3.25 us (2%)
  local copies, waits for them, and re-layouts  2.99 us (2%)
    all_gather x1, blocking collectives, shards(): line = lax.all_gather(factor, 'z', axis=0, tiled=True)  29.6 us
    all_to_all x1, blocking collectives, shards(): picked = lax.all_to_all(picked, PLANE, 0, 0, tiled=True)  28.1 us
    all_to_all x1, starting transfers between devices, shards(): lax.all_to_all(jnp.broadcast_to(block_map, (16, 2)), PLANE, 0, 0, tiled=T...  17.4 us
    all_to_all x1, waiting for transfers between devices, shards(): quarters = lax.all_to_all(partial_sum, 'yh', 0, 0, tiled=True)  13.9 us
    all_gather x1, blocking collectives, shards(): lax.all_gather(coulomb.astype(jnp.bfloat16), 'yh', axis=0, tiled=True)  13.6 us
    all_to_all x1, waiting for transfers between devices, shards(): lax.all_to_all(near_sum, ('yl', 'z'), 0, 0, tiled=True)  13 us
    all_to_all x1, starting transfers between devices, shards(): ordered = lax.all_to_all(ordered, ('x', 'core'), 0, 0, tiled=True)  10.1 us
    all_to_all x1, waiting for transfers between devices, shards(): ordered = lax.all_to_all(ordered, ('x', 'core'), 0, 0, tiled=True)  7.88 us
  transfers between devices with their start and end apart: 4, of which 3 were waited for; matrix products, arithmetic and copies ran while one was open for 1% of the time, Pallas kernels for 0%

profile of v5, /device:TPU:1, one launch (start us, length us, event | category | flops | bytes accessed | tf_op | source)
XLA Modules:
  0.0 157.2 jit_solution(17876005824604051690)
XLA Ops:
  0.0 1.3 broadcast_in_dim.63
  1.3 17.4 %all-to-all-start = ((s32[16,1,2]{2,1,0:T(1,128)}), s32[16,1,2]{2,1,0:T(1,128)S(1)}, u32[]{:S(2)}, u32[]{:S(2)}) async-start(s32[16,1,2]{2,1,0:T(1,128)} %broadcast_in_dim.63), calls=%async_computation | async-start | bytes 16384 | tf_op jit(solution)/shard_map/all_to_all | solution.py:157
  18.7 29.6 %all_gather.6 = bf16[32,16,704]{2,1,0:T(8,128)(2,1)S(1)} all-gather(bf16[2,16,704]{2,1,0:T(8,128)(2,1)} %param.7), channel_id=1, replica_groups=mesh['yl'=2,'x'=4,'z'=16,'core'=2,'yh'=4] {'z'}, dimensions={0}, use_global_device_ids=true | all-gather | bytes 765952 | tf_op jit(solution)/shard_map/all_gather | solution.py:160
  48.3 0.2 copy.13
  48.8 1.0 fusion.2
  49.8 28.1 %all_to_all.26.picked_ref = bf16[16,64,512]{2,1,0:T(8,128)(2,1)S(1)} all-to-all(bf16[16,64,512]{2,1,0:T(8,128)(2,1)S(1)} %bitcast.7), channel_id=1, replica_groups=mesh['yl'=2,'x'=4,'z'=16,'core'=2,'yh'=4] {'yl','x','core'}, dimensions={0} | all-to-all | bytes 2097152 | tf_op jit(solution)/shard_map/all_to_all | solution.py:168
  77.9 2.3 %block_integrals.1 = f32[16,16,1152]{2,1,0:T(8,128)S(1)} custom-call(bf16[16,64,512]{2,1,0:T(8,128)(2,1)S(1)} %all_to_all.26.picked_ref), custom_call_target="tpu_custom_call" | custom-call | flops 268435456 | bytes 2097152 | tf_op jit(solution)/shard_map/block_integrals/pallas_call | solution.py:118
  80.2 0.9 convert_element_type.17
  81.0 5.9 %all-to-all-start.2 = ((f16[4,64,1152]{2,1,0:T(8,128)(2,1)}), f16[4,64,1152]{2,1,0:T(8,128)(2,1)}, u32[]{:S(2)}, u32[]{:S(2)}) async-start(f16[4,64,1152]{2,1,0:T(8,128)(2,1)} %bitcast.4), calls=%async_computation.2 | async-start | bytes 1179648 | tf_op jit(solution)/shard_map/all_to_all | solution.py:170
  87.0 13.9 %all-to-all-done.2 = f16[4,64,1152]{2,1,0:T(8,128)(2,1)} async-done(((f16[4,64,1152]{2,1,0:T(8,128)(2,1)}), f16[4,64,1152]{2,1,0:T(8,128)(2,1)}, u32[]{:S(2)}, u32[]{:S(2)}) %all-to-all-start.2) | async-done | bytes 589856 | tf_op jit(solution)/shard_map/all_to_all | solution.py:170
  100.9 1.1 convert_element_type.18
  102.0 0.1 fusion.13
  102.2 0.1 fusion.3
  102.3 13.6 %all_gather.7.mirrored_ref = bf16[256,1024]{1,0:T(8,128)(2,1)S(1)} all-gather(bf16[64,1024]{1,0:T(8,128)(2,1)S(1)} %fusion.3), channel_id=1, replica_groups=mesh['yl'=2,'x'=4,'z'=16,'core'=2,'yh'=4] {'yh'}, dimensions={0}, use_global_device_ids=true | all-gather | bytes 655360 | tf_op jit(solution)/shard_map/all_gather | solution.py:174
  116.0 2.1 %residual_terms.1 = bf16[8,96,256]{2,1,0:T(8,128)(2,1)} custom-call(bf16[1,768,1024]{2,1,0:T(8,128)(2,1)S(1)} %copy-done, bf16[1,768,1024]{2,1,0:T(8,128)(2,1)S(1)} %copy-done.1, bf16[256,1024]{1,0:T(8,128)(2,1)S(1)} %all_gather.7.mirrored_ref), custom_call_target="tpu_custom_call" | custom-call | flops 805306368 | bytes 4194304 | tf_op jit(solution)/shard_map/residual_terms/pallas_call | solution.py:102
  118.1 10.1 %all-to-all-start.3 = ((bf16[8,96,256]{2,1,0:T(8,128)(2,1)}), bf16[8,96,256]{2,1,0:T(8,128)(2,1)S(1)}, u32[]{:S(2)}, u32[]{:S(2)}) async-start(bf16[8,96,256]{2,1,0:T(8,128)(2,1)} %residual_terms.1), calls=%async_computation.3 | async-start | bytes 786432 | tf_op jit(solution)/shard_map/all_to_all | solution.py:176
  128.2 0.1 select_reduce_fusion.1
  128.3 7.9 %all-to-all-done.3 = bf16[8,96,256]{2,1,0:T(8,128)(2,1)S(1)} async-done(((bf16[8,96,256]{2,1,0:T(8,128)(2,1)}), bf16[8,96,256]{2,1,0:T(8,128)(2,1)S(1)}, u32[]{:S(2)}, u32[]{:S(2)}) %all-to-all-start.3) | async-done | bytes 393248 | tf_op jit(solution)/shard_map/all_to_all | solution.py:176
  136.3 0.7 reshape.144
  137.0 6.0 %all-to-all-start.4 = ((f32[32,1,768]{2,1,0:T(1,128)}), f32[32,1,768]{2,1,0:T(1,128)S(1)}, u32[]{:S(2)}, u32[]{:S(2)}) async-start(f32[32,1,768]{2,1,0:T(1,128)} %reshape.144), calls=%async_computation.4 | async-start | bytes 196608 | tf_op jit(solution)/shard_map/all_to_all | solution.py:178
  143.0 0.1 select_reduce_fusion.4
  143.1 0.5 select_reduce_fusion
  143.6 13.0 %all-to-all-done.4 = f32[32,1,768]{2,1,0:T(1,128)S(1)} async-done(((f32[32,1,768]{2,1,0:T(1,128)}), f32[32,1,768]{2,1,0:T(1,128)S(1)}, u32[]{:S(2)}, u32[]{:S(2)}) %all-to-all-start.4) | async-done | bytes 98336 | tf_op jit(solution)/shard_map/all_to_all | solution.py:178
  156.6 0.6 div.45
  (22 shorter events, 0.5 us)
Async XLA Ops:
  1.3 47.3 %all-to-all-start = ((s32[16,1,2]{2,1,0:T(1,128)}), s32[16,1,2]{2,1,0:T(1,128)S(1)}, u32[]{:S(2)}, u32[]{:S(2)}) async-start(s32[16,1,2]{2,1,0:T(1,128)} %broadcast_in_dim.63), calls=%async_computation | async-start | bytes 16384 | tf_op jit(solution)/shard_map/all_to_all | solution.py:157
  81.0 19.8 %all-to-all-start.2 = ((f16[4,64,1152]{2,1,0:T(8,128)(2,1)}), f16[4,64,1152]{2,1,0:T(8,128)(2,1)}, u32[]{:S(2)}, u32[]{:S(2)}) async-start(f16[4,64,1152]{2,1,0:T(8,128)(2,1)} %bitcast.4), calls=%async_computation.2 | async-start | bytes 1179648 | tf_op jit(solution)/shard_map/all_to_all | solution.py:170
  87.0 29.0 %copy-start = (bf16[1,768,1024]{2,1,0:T(8,128)(2,1)S(1)}, bf16[1,768,1024]{2,1,0:T(8,128)(2,1)}, u32[]{:S(2)}) copy-start(bf16[1,768,1024]{2,1,0:T(8,128)(2,1)} %forward_ref.1) | copy-start | bytes 4718596
  87.0 29.0 %copy-start.1 = (bf16[1,768,1024]{2,1,0:T(8,128)(2,1)S(1)}, bf16[1,768,1024]{2,1,0:T(8,128)(2,1)}, u32[]{:S(2)}) copy-start(bf16[1,768,1024]{2,1,0:T(8,128)(2,1)} %reversed_ref.1) | copy-start | bytes 4718596
  115.9 12.2 %copy-start.2 = (s32[768,2]{0,1:T(2,128)S(1)}, s32[768,2]{0,1:T(2,128)}, u32[]{:S(2)}) copy-start(s32[768,2]{0,1:T(2,128)} %param.11) | copy-start | bytes 18436
  115.9 12.2 %copy-start.3 = (f32[64]{0:T(128)S(1)}, f32[64]{0:T(128)}, u32[]{:S(2)}) copy-start(f32[64]{0:T(128)} %param.13) | copy-start | bytes 772
  118.1 25.0 %copy-start.4 = (f32[16]{0:T(128)S(1)}, f32[16]{0:T(128)}, u32[]{:S(2)}) copy-start(f32[16]{0:T(128)} %param.12) | copy-start | bytes 196
  118.1 18.2 %all-to-all-start.3 = ((bf16[8,96,256]{2,1,0:T(8,128)(2,1)}), bf16[8,96,256]{2,1,0:T(8,128)(2,1)S(1)}, u32[]{:S(2)}, u32[]{:S(2)}) async-start(bf16[8,96,256]{2,1,0:T(8,128)(2,1)} %residual_terms.1), calls=%async_computation.3 | async-start | bytes 786432 | tf_op jit(solution)/shard_map/all_to_all | solution.py:176
  137.0 19.5 %all-to-all-start.4 = ((f32[32,1,768]{2,1,0:T(1,128)}), f32[32,1,768]{2,1,0:T(1,128)S(1)}, u32[]{:S(2)}, u32[]{:S(2)}) async-start(f32[32,1,768]{2,1,0:T(1,128)} %reshape.144), calls=%async_computation.4 | async-start | bytes 196608 | tf_op jit(solution)/shard_map/all_to_all | solution.py:178

commit v6 on v5

--- a/solution.py
+++ b/solution.py
@@ -93,15 +93,14 @@
     hot = (col == line * 3 + within + core * 3).astype(jnp.bfloat16)
     for at in range(8):
         ordered = select_matmul(hot, term_ref[at * piece : (at + 1) * piece])
-        rows = slice(at // 4 * (piece // 2), (at // 4 + 1) * (piece // 2))
-        out_ref[at % 4 * 2, rows] = ordered[: piece // 2]
-        out_ref[at % 4 * 2 + 1, rows] = ordered[piece // 2 :]
+        out_ref[at * 2] = ordered[: piece // 2]
+        out_ref[at * 2 + 1] = ordered[piece // 2 :]
 
 
 def residual_terms(forward, backward, mirrored):
     return pl.pallas_call(
         residual_kernel,
-        out_shape=jax.ShapeDtypeStruct((8, 96, AW * AW), jnp.bfloat16),
+        out_shape=jax.ShapeDtypeStruct((16, 48, AW * AW), jnp.bfloat16),
         in_specs=[pl.BlockSpec(memory_space=pltpu.VMEM)] * 3,
         out_specs=pl.BlockSpec(memory_space=pltpu.VMEM),
         scratch_shapes=[pltpu.VMEM((768, AW * AW), jnp.bfloat16)],
@@ -173,9 +172,9 @@
     coulomb = jnp.sum(quarters[:, :, :PAIRS] * unscale, axis=0)
     mirrored = lax.all_gather(coulomb.astype(jnp.bfloat16), "yh", axis=0, tiled=True)
     ordered = residual_terms(amplitude_forward, amplitude_reversed, mirrored)
-    ordered = lax.all_to_all(ordered, ("x", "core"), 0, 0, tiled=True)
-    near_sum = jnp.sum(ordered.astype(jnp.float32), axis=0).reshape(32, 1, 768)
-    owned = jnp.sum(lax.all_to_all(near_sum, ("yl", "z"), 0, 0, tiled=True), axis=0)
+    ordered = lax.all_to_all(ordered, PLANE, 0, 0, tiled=True)
+    plane_sum = jnp.sum(ordered.astype(jnp.float32), axis=0).reshape(16, 1, 768)
+    owned = jnp.sum(lax.all_to_all(plane_sum, "z", 0, 0, tiled=True), axis=0)
 
     owned_len = owned.shape[1]
     offset = lax.axis_index(BLK) * owned_len

time: 158 us -> 153 us (0.968)
  blocking collectives: 71.3 us -> 92.1 us
  waiting for transfers between devices: 34.8 us -> 19.1 us
  starting transfers between devices: 39.4 us -> 31.7 us
  other arithmetic: 3.25 us -> 1.34 us
    all_to_all x0 -> x1, blocking collectives: none -> 20 us  [shards(): quarters = lax.all_to_all(partial_sum, 'yh', 0, 0, tiled=True)]
    all_to_all x3 -> x2, waiting for transfers between devices: 34.8 us -> 19.1 us  [the longest x1 11 us: shards(): owned = jnp.sum(lax.all_to_all(plane_sum, 'z', 0, 0, tiled=True), axis=0)]
    all_to_all x3 -> x2, starting transfers between devices: 22 us -> 14.2 us  [the longest x1 10.7 us: shards(): ordered = lax.all_to_all(ordered, PLANE, 0, 0, tiled=True)]
  transfers between devices with their start and end apart: 4 -> 3, of which waited for: 3 -> 2; matrix products, arithmetic and copies ran while one was open for 1% -> 1% of each run, Pallas kernels for 0% -> 0%
where the time goes in v6:
time: 153 us
  blocking collectives  92.1 us (60%)
  starting transfers between devices  31.7 us (21%)
  waiting for transfers between devices  19.1 us (12%)
  Pallas kernels  4.37 us (3%)
  local copies, waits for them, and re-layouts  2.94 us (2%)
    all_gather x1, blocking collectives, shards(): line = lax.all_gather(factor, 'z', axis=0, tiled=True)  29.6 us
    all_to_all x1, blocking collectives, shards(): picked = lax.all_to_all(picked, PLANE, 0, 0, tiled=True)  28.1 us
    all_to_all x1, blocking collectives, shards(): quarters = lax.all_to_all(partial_sum, 'yh', 0, 0, tiled=True)  20 us
    all_to_all x1, starting transfers between devices, shards(): lax.all_to_all(jnp.broadcast_to(block_map, (16, 2)), PLANE, 0, 0, tiled=T...  17.4 us
    all_gather x1, blocking collectives, shards(): lax.all_gather(coulomb.astype(jnp.bfloat16), 'yh', axis=0, tiled=True)  14.4 us
    all_to_all x1, waiting for transfers between devices, shards(): owned = jnp.sum(lax.all_to_all(plane_sum, 'z', 0, 0, tiled=True), axis=0)  11 us
    all_to_all x1, starting transfers between devices, shards(): ordered = lax.all_to_all(ordered, PLANE, 0, 0, tiled=True)  10.7 us
    all_to_all x1, waiting for transfers between devices, shards(): ordered = lax.all_to_all(ordered, PLANE, 0, 0, tiled=True)  8.16 us
  transfers between devices with their start and end apart: 3, of which 2 were waited for; matrix products, arithmetic and copies ran while one was open for 1% of the time, Pallas kernels for 0%

profile of v6, /device:TPU:1, one launch (start us, length us, event | category | flops | bytes accessed | tf_op | source)
XLA Modules:
  0.0 152.8 jit_solution(9933632096728975011)
XLA Ops:
  0.0 1.3 broadcast_in_dim.63
  1.3 17.4 %all-to-all-start = ((s32[16,1,2]{2,1,0:T(1,128)}), s32[16,1,2]{2,1,0:T(1,128)S(1)}, u32[]{:S(2)}, u32[]{:S(2)}) async-start(s32[16,1,2]{2,1,0:T(1,128)} %broadcast_in_dim.63), calls=%async_computation | async-start | bytes 16384 | tf_op jit(solution)/shard_map/all_to_all | solution.py:156
  18.7 29.6 %all_gather.6 = bf16[32,16,704]{2,1,0:T(8,128)(2,1)S(1)} all-gather(bf16[2,16,704]{2,1,0:T(8,128)(2,1)} %param.7), channel_id=1, replica_groups=mesh['yl'=2,'x'=4,'z'=16,'core'=2,'yh'=4] {'z'}, dimensions={0}, use_global_device_ids=true | all-gather | bytes 765952 | tf_op jit(solution)/shard_map/all_gather | solution.py:159
  48.3 0.2 copy.13
  48.5 0.1 mul.38
  48.7 0.1 add.87
  48.8 1.0 fusion.2
  49.8 28.1 %all_to_all.26.picked_ref = bf16[16,64,512]{2,1,0:T(8,128)(2,1)S(1)} all-to-all(bf16[16,64,512]{2,1,0:T(8,128)(2,1)S(1)} %bitcast.8), channel_id=1, replica_groups=mesh['yl'=2,'x'=4,'z'=16,'core'=2,'yh'=4] {'yl','x','core'}, dimensions={0} | all-to-all | bytes 2097152 | tf_op jit(solution)/shard_map/all_to_all | solution.py:167
  77.9 2.3 %block_integrals.1 = f32[16,16,1152]{2,1,0:T(8,128)S(1)} custom-call(bf16[16,64,512]{2,1,0:T(8,128)(2,1)S(1)} %all_to_all.26.picked_ref), custom_call_target="tpu_custom_call" | custom-call | flops 268435456 | bytes 2097152 | tf_op jit(solution)/shard_map/block_integrals/pallas_call | solution.py:117
  80.2 20.0 %all_to_all.27 = f16[4,64,1152]{2,1,0:T(8,128)(2,1)S(1)} all-to-all(f16[4,64,1152]{2,1,0:T(8,128)(2,1)S(1)} %bitcast.7), channel_id=1, replica_groups=mesh['yl'=2,'x'=4,'z'=16,'core'=2,'yh'=4] {'yh'}, dimensions={0} | all-to-all | bytes 1179648 | tf_op jit(solution)/shard_map/all_to_all | solution.py:169
  100.3 0.1 convert_element_type.18
  100.4 0.1 fusion.13
  100.5 0.1 fusion.3
  100.7 14.4 %all_gather.7.mirrored_ref = bf16[256,1024]{1,0:T(8,128)(2,1)S(1)} all-gather(bf16[64,1024]{1,0:T(8,128)(2,1)S(1)} %fusion.3), channel_id=1, replica_groups=mesh['yl'=2,'x'=4,'z'=16,'core'=2,'yh'=4] {'yh'}, dimensions={0}, use_global_device_ids=true | all-gather | bytes 655360 | tf_op jit(solution)/shard_map/all_gather | solution.py:173
  115.1 2.1 %residual_terms.1 = bf16[16,48,256]{2,1,0:T(8,128)(2,1)} custom-call(bf16[1,768,1024]{2,1,0:T(8,128)(2,1)S(1)} %copy-done, bf16[1,768,1024]{2,1,0:T(8,128)(2,1)S(1)} %copy-done.1, bf16[256,1024]{1,0:T(8,128)(2,1)S(1)} %all_gather.7.mirrored_ref), custom_call_target="tpu_custom_call" | custom-call | flops 805306368 | bytes 4194304 | tf_op jit(solution)/shard_map/residual_terms/pallas_call | solution.py:101
  117.2 10.7 %all-to-all-start.3 = ((bf16[16,48,256]{2,1,0:T(8,128)(2,1)}), bf16[16,48,256]{2,1,0:T(8,128)(2,1)S(1)}, u32[]{:S(2)}, u32[]{:S(2)}) async-start(bf16[16,48,256]{2,1,0:T(8,128)(2,1)} %residual_terms.1), calls=%async_computation.3 | async-start | bytes 786432 | tf_op jit(solution)/shard_map/all_to_all | solution.py:175
  128.0 0.1 select_reduce_fusion.4
  128.2 0.1 select_reduce_fusion.1
  128.3 8.2 %all-to-all-done.3 = bf16[16,48,256]{2,1,0:T(8,128)(2,1)S(1)} async-done(((bf16[16,48,256]{2,1,0:T(8,128)(2,1)}), bf16[16,48,256]{2,1,0:T(8,128)(2,1)S(1)}, u32[]{:S(2)}, u32[]{:S(2)}) %all-to-all-start.3) | async-done | bytes 393248 | tf_op jit(solution)/shard_map/all_to_all | solution.py:175
  136.5 0.7 reshape.144
  137.2 3.5 %all-to-all-start.4 = ((f32[16,1,768]{2,1,0:T(1,128)}), f32[16,1,768]{2,1,0:T(1,128)S(1)}, u32[]{:S(2)}, u32[]{:S(2)}) async-start(f32[16,1,768]{2,1,0:T(1,128)} %reshape.144), calls=%async_computation.4 | async-start | bytes 98304 | tf_op jit(solution)/shard_map/all_to_all | solution.py:177
  140.7 0.5 select_reduce_fusion
  141.2 11.0 %all-to-all-done.4 = f32[16,1,768]{2,1,0:T(1,128)S(1)} async-done(((f32[16,1,768]{2,1,0:T(1,128)}), f32[16,1,768]{2,1,0:T(1,128)S(1)}, u32[]{:S(2)}, u32[]{:S(2)}) %all-to-all-start.4) | async-done | bytes 49184 | tf_op jit(solution)/shard_map/all_to_all | solution.py:177
  152.2 0.6 div.45
  (21 shorter events, 0.4 us)
Async XLA Ops:
  1.3 47.3 %all-to-all-start = ((s32[16,1,2]{2,1,0:T(1,128)}), s32[16,1,2]{2,1,0:T(1,128)S(1)}, u32[]{:S(2)}, u32[]{:S(2)}) async-start(s32[16,1,2]{2,1,0:T(1,128)} %broadcast_in_dim.63), calls=%async_computation | async-start | bytes 16384 | tf_op jit(solution)/shard_map/all_to_all | solution.py:156
  100.3 14.8 %copy-start = (bf16[1,768,1024]{2,1,0:T(8,128)(2,1)S(1)}, bf16[1,768,1024]{2,1,0:T(8,128)(2,1)}, u32[]{:S(2)}) copy-start(bf16[1,768,1024]{2,1,0:T(8,128)(2,1)} %forward_ref.1) | copy-start | bytes 4718596
  100.3 14.8 %copy-start.1 = (bf16[1,768,1024]{2,1,0:T(8,128)(2,1)S(1)}, bf16[1,768,1024]{2,1,0:T(8,128)(2,1)}, u32[]{:S(2)}) copy-start(bf16[1,768,1024]{2,1,0:T(8,128)(2,1)} %reversed_ref.1) | copy-start | bytes 4718596
  115.1 12.9 %copy-start.2 = (s32[768,2]{0,1:T(2,128)S(1)}, s32[768,2]{0,1:T(2,128)}, u32[]{:S(2)}) copy-start(s32[768,2]{0,1:T(2,128)} %param.11) | copy-start | bytes 18436
  115.1 12.9 %copy-start.3 = (f32[16]{0:T(128)S(1)}, f32[16]{0:T(128)}, u32[]{:S(2)}) copy-start(f32[16]{0:T(128)} %param.12) | copy-start | bytes 196
  115.1 13.0 %copy-start.4 = (f32[64]{0:T(128)S(1)}, f32[64]{0:T(128)}, u32[]{:S(2)}) copy-start(f32[64]{0:T(128)} %param.13) | copy-start | bytes 772
  117.2 19.2 %all-to-all-start.3 = ((bf16[16,48,256]{2,1,0:T(8,128)(2,1)}), bf16[16,48,256]{2,1,0:T(8,128)(2,1)S(1)}, u32[]{:S(2)}, u32[]{:S(2)}) async-start(bf16[16,48,256]{2,1,0:T(8,128)(2,1)} %residual_terms.1), calls=%async_computation.3 | async-start | bytes 786432 | tf_op jit(solution)/shard_map/all_to_all | solution.py:175
  137.2 15.0 %all-to-all-start.4 = ((f32[16,1,768]{2,1,0:T(1,128)}), f32[16,1,768]{2,1,0:T(1,128)S(1)}, u32[]{:S(2)}, u32[]{:S(2)}) async-start(f32[16,1,768]{2,1,0:T(1,128)} %reshape.144), calls=%async_computation.4 | async-start | bytes 98304 | tf_op jit(solution)/shard_map/all_to_all | solution.py:177

commit v7 on v6

--- a/solution.py
+++ b/solution.py
@@ -9,7 +9,8 @@
 AW = 16
 BLOCK_VIRTUALS = 32
 NV = 704
-BLK = ("yl", "x", "z", "core")
+BLK = ("yl", "x", "z8", "zp", "core")
+NEAR = ("yl", "x", "zp", "core")
 PLANE = ("yl", "x", "core")
 GROUP = 4
 LANES = 128
@@ -17,29 +18,32 @@
 TOP = 14.0
 
 
-def swap_lane_blocks(tiles):
+def swap_lane_blocks(tiles, width):
+    tiles = list(tiles)
     lane = lax.broadcasted_iota(jnp.int32, tiles[0].shape, 1)
-    block = lax.shift_right_logical(lane, 5)
-    result = []
-    for j in range(GROUP):
-        out = None
-        for i in range(GROUP):
-            shift = (i - j) * BLOCK_VIRTUALS % LANES
-            moved = pltpu.roll(tiles[i], shift, 1) if shift else tiles[i]
-            out = moved if out is None else jnp.where(block == i, moved, out)
-        result.append(out)
-    return result
+    step = 1
+    while step < len(tiles):
+        low = lax.bitwise_and(lane, step * width) == 0
+        for i in range(len(tiles)):
+            if i & step == 0:
+                first, second = tiles[i], tiles[i + step]
+                tiles[i] = jnp.where(low, first, pltpu.roll(second, step * width, 1))
+                tiles[i + step] = jnp.where(
+                    low, pltpu.roll(first, LANES - step * width, 1), second
+                )
+        step *= 2
+    return tiles
 
 
 def integrals_kernel(picked_ref, out_ref, left_ref, right_ref, product_ref):
-    for source in range(0, 16, GROUP):
-        for first in range(0, AW, GROUP):
-            lanes = slice(first * BLOCK_VIRTUALS, first * BLOCK_VIRTUALS + LANES)
-            tiles = [
-                picked_ref[source + i, :, lanes].astype(jnp.float32) for i in range(GROUP)
-            ]
-            depth = slice(source * BLOCK_VIRTUALS, source * BLOCK_VIRTUALS + LANES)
-            for j, tile in enumerate(swap_lane_blocks(tiles)):
+    q_line = picked_ref.shape[2] // AW
+    count = LANES // q_line
+    for source in range(0, picked_ref.shape[0], count):
+        for first in range(0, AW, count):
+            lanes = slice(first * q_line, first * q_line + LANES)
+            tiles = [picked_ref[source + i, :, lanes].astype(jnp.float32) for i in range(count)]
+            depth = slice(source * q_line, source * q_line + LANES)
+            for j, tile in enumerate(swap_lane_blocks(tiles, q_line)):
                 rows = slice((first + j) * BLOCK_VIRTUALS, (first + j + 1) * BLOCK_VIRTUALS)
                 tile = tile.astype(jnp.bfloat16)
                 left_ref[rows, depth] = tile[:BLOCK_VIRTUALS]
@@ -59,7 +63,7 @@
         for b in range(0, AW, GROUP):
             lanes = slice(b * BLOCK_VIRTUALS, b * BLOCK_VIRTUALS + LANES)
             tiles = [product_ref[:, c + i, lanes] for i in range(GROUP)]
-            for j, tile in enumerate(swap_lane_blocks(tiles)):
+            for j, tile in enumerate(swap_lane_blocks(tiles, BLOCK_VIRTUALS)):
                 lanes_out = slice(c * BLOCK_VIRTUALS, c * BLOCK_VIRTUALS + LANES)
                 out_ref[b + j, :, lanes_out] = tile
 
@@ -154,17 +158,17 @@
     factor, amplitude_forward, amplitude_reversed, block_map, pair_list, virt_energy, occ_energy
 ):
     plane_map = lax.all_to_all(
-        jnp.broadcast_to(block_map, (16, 2)), PLANE, 0, 0, tiled=True
-    )
-    line = lax.all_gather(factor, "z", axis=0, tiled=True)
+        jnp.broadcast_to(block_map, (32, 2)), NEAR, 0, 0, tiled=True
+    )
+    line = lax.all_gather(factor, "z8", axis=0, tiled=True)
     q_line = line.shape[0]
     wanted = (
         plane_map.reshape(-1, 1) * BLOCK_VIRTUALS + jnp.arange(BLOCK_VIRTUALS, dtype=jnp.int32)
     ).reshape(-1)
     line = line.transpose(1, 0, 2).reshape(AW * q_line, NV)
     picked = select_rows(one_hot_rows(wanted, NV), line)
-    picked = picked.reshape(16, 2 * BLOCK_VIRTUALS, AW * q_line)
-    picked = lax.all_to_all(picked, PLANE, 0, 0, tiled=True)
+    picked = picked.reshape(32, 2 * BLOCK_VIRTUALS, AW * q_line)
+    picked = lax.all_to_all(picked, NEAR, 0, 0, tiled=True)
     partial_sum = block_integrals(picked).astype(jnp.float16).reshape(4, 4 * AW, -1)
     quarters = lax.all_to_all(partial_sum, "yh", 0, 0, tiled=True)
     quarters = quarters.astype(jnp.float32)
@@ -174,7 +178,7 @@
     ordered = residual_terms(amplitude_forward, amplitude_reversed, mirrored)
     ordered = lax.all_to_all(ordered, PLANE, 0, 0, tiled=True)
     plane_sum = jnp.sum(ordered.astype(jnp.float32), axis=0).reshape(16, 1, 768)
-    owned = jnp.sum(lax.all_to_all(plane_sum, "z", 0, 0, tiled=True), axis=0)
+    owned = jnp.sum(lax.all_to_all(plane_sum, ("z8", "zp"), 0, 0, tiled=True), axis=0)
 
     owned_len = owned.shape[1]
     offset = lax.axis_index(BLK) * owned_len
@@ -192,7 +196,7 @@
 
 
 def solution(mesh):
-    fine = Mesh(mesh.devices.reshape(2, 4, 16, 2, 4), BLK + ("yh",))
+    fine = Mesh(mesh.devices.reshape(2, 4, 8, 2, 2, 4), BLK + ("yh",))
     placed = (
         P(BLK + ("yh",), None, None),
         P(BLK, "yh", None),

time: 153 us -> 157 us (1.026)
  Pallas kernels: 4.37 us -> 6.64 us
    all_to_all x1, starting transfers between devices: 10.7 us -> 7.46 us  [shards(): ordered = lax.all_to_all(ordered, PLANE, 0, 0, tiled=True)]
    all_to_all x1, blocking collectives: 20 us -> 23.3 us  [shards(): quarters = lax.all_to_all(partial_sum, 'yh', 0, 0, tiled=True)]
    all_to_all x2, starting transfers between devices: 20.9 us -> 24 us  [the longest x1 17.7 us: shards(): lax.all_to_all(jnp.broadcast_to(block_map, (32, 2)), NEAR, 0, 0, tiled=True)]
    all_gather x1, blocking collectives: 29.6 us -> 26.8 us  [shards(): line = lax.all_gather(factor, 'z8', axis=0, tiled=True)]
    pallas_call x1, Pallas kernels: 2.26 us -> 4.54 us  [block_integrals(): pl.pallas_call(integrals_kernel, out_shape=jax.ShapeDtypeStruct((AW, AW,...]
where the time goes in v7:
time: 157 us; the launch traced here: 156 us
  blocking collectives  92.6 us (59%)
  starting transfers between devices  31.4 us (20%)
  waiting for transfers between devices  19.2 us (12%)
  Pallas kernels  6.64 us (4%)
  local copies, waits for them, and re-layouts  2.85 us (2%)
    all_to_all x1, blocking collectives, shards(): picked = lax.all_to_all(picked, NEAR, 0, 0, tiled=True)  29.3 us
    all_gather x1, blocking collectives, shards(): line = lax.all_gather(factor, 'z8', axis=0, tiled=True)  26.8 us
    all_to_all x1, blocking collectives, shards(): quarters = lax.all_to_all(partial_sum, 'yh', 0, 0, tiled=True)  23.3 us
    all_to_all x1, starting transfers between devices, shards(): lax.all_to_all(jnp.broadcast_to(block_map, (32, 2)), NEAR, 0, 0, tiled=True)  17.7 us
    all_gather x1, blocking collectives, shards(): lax.all_gather(coulomb.astype(jnp.bfloat16), 'yh', axis=0, tiled=True)  13.1 us
    all_to_all x1, waiting for transfers between devices, shards(): lax.all_to_all(plane_sum, ('z8', 'zp'), 0, 0, tiled=True)  11.2 us
    all_to_all x1, waiting for transfers between devices, shards(): ordered = lax.all_to_all(ordered, PLANE, 0, 0, tiled=True)  8.08 us
    all_to_all x1, starting transfers between devices, shards(): ordered = lax.all_to_all(ordered, PLANE, 0, 0, tiled=True)  7.46 us
  transfers between devices with their start and end apart: 3, of which 2 were waited for; matrix products, arithmetic and copies ran while one was open for 1% of the time, Pallas kernels for 0%

profile of v7, /device:TPU:1, one launch (start us, length us, event | category | flops | bytes accessed | tf_op | source)
XLA Modules:
  0.0 155.8 jit_solution(17851053046602542409)
XLA Ops:
  0.0 1.3 broadcast_in_dim.63
  1.3 17.7 %all-to-all-start = ((s32[32,1,2]{2,1,0:T(1,128)}), s32[32,1,2]{2,1,0:T(1,128)S(1)}, u32[]{:S(2)}, u32[]{:S(2)}) async-start(s32[32,1,2]{2,1,0:T(1,128)} %broadcast_in_dim.63), calls=%async_computation | async-start | bytes 32768 | tf_op jit(solution)/shard_map/all_to_all | solution.py:160
  18.9 26.8 %all_gather.6 = bf16[16,16,704]{2,1,0:T(8,128)(2,1)S(1)} all-gather(bf16[2,16,704]{2,1,0:T(8,128)(2,1)} %param.7), channel_id=1, replica_groups=mesh['yl'=2,'x'=4,'z8'=8,'zp'=2,'core'=2,'yh'=4] {'z8'}, dimensions={0}, use_global_device_ids=true | all-gather | bytes 405504 | tf_op jit(solution)/shard_map/all_gather | solution.py:163
  45.8 0.1 copy.13
  45.9 0.1 mul.41
  46.1 0.1 add.90
  46.2 1.5 fusion.2
  47.7 29.3 %all_to_all.26.picked_ref = bf16[32,64,256]{2,1,0:T(8,128)(2,1)S(1)} all-to-all(bf16[32,64,256]{2,1,0:T(8,128)(2,1)S(1)} %bitcast.8), channel_id=1, replica_groups=mesh['yl'=2,'x'=4,'z8'=8,'zp'=2,'core'=2,'yh'=4] {'yl','x','zp','core'}, dimensions={0} | all-to-all | bytes 2097152 | tf_op jit(solution)/shard_map/all_to_all | solution.py:171
  77.0 4.5 %block_integrals.1 = f32[16,16,1152]{2,1,0:T(8,128)S(1)} custom-call(bf16[32,64,256]{2,1,0:T(8,128)(2,1)S(1)} %all_to_all.26.picked_ref), custom_call_target="tpu_custom_call" | custom-call | flops 268435456 | bytes 2097152 | tf_op jit(solution)/shard_map/block_integrals/pallas_call | solution.py:121
  81.6 23.3 %all_to_all.27 = f16[4,64,1152]{2,1,0:T(8,128)(2,1)S(1)} all-to-all(f16[4,64,1152]{2,1,0:T(8,128)(2,1)S(1)} %bitcast.6), channel_id=1, replica_groups=mesh['yl'=2,'x'=4,'z8'=8,'zp'=2,'core'=2,'yh'=4] {'yh'}, dimensions={0} | all-to-all | bytes 1179648 | tf_op jit(solution)/shard_map/all_to_all | solution.py:173
  104.9 0.1 convert_element_type.18
  105.0 0.1 fusion.13
  105.1 0.1 fusion.3
  105.3 13.1 %all_gather.7.mirrored_ref = bf16[256,1024]{1,0:T(8,128)(2,1)S(1)} all-gather(bf16[64,1024]{1,0:T(8,128)(2,1)S(1)} %fusion.3), channel_id=1, replica_groups=mesh['yl'=2,'x'=4,'z8'=8,'zp'=2,'core'=2,'yh'=4] {'yh'}, dimensions={0}, use_global_device_ids=true | all-gather | bytes 655360 | tf_op jit(solution)/shard_map/all_gather | solution.py:177
  118.5 2.1 %residual_terms.1 = bf16[16,48,256]{2,1,0:T(8,128)(2,1)} custom-call(bf16[1,768,1024]{2,1,0:T(8,128)(2,1)S(1)} %copy-done, bf16[1,768,1024]{2,1,0:T(8,128)(2,1)S(1)} %copy-done.1, bf16[256,1024]{1,0:T(8,128)(2,1)S(1)} %all_gather.7.mirrored_ref), custom_call_target="tpu_custom_call" | custom-call | flops 805306368 | bytes 4194304 | tf_op jit(solution)/shard_map/residual_terms/pallas_call | solution.py:105
  120.6 7.5 %all-to-all-start.3 = ((bf16[16,48,256]{2,1,0:T(8,128)(2,1)}), bf16[16,48,256]{2,1,0:T(8,128)(2,1)S(1)}, u32[]{:S(2)}, u32[]{:S(2)}) async-start(bf16[16,48,256]{2,1,0:T(8,128)(2,1)} %residual_terms.1), calls=%async_computation.3 | async-start | bytes 786432 | tf_op jit(solution)/shard_map/all_to_all | solution.py:179
  128.1 0.1 select_reduce_fusion.4
  128.2 0.1 select_reduce_fusion.1
  128.3 8.1 %all-to-all-done.3 = bf16[16,48,256]{2,1,0:T(8,128)(2,1)S(1)} async-done(((bf16[16,48,256]{2,1,0:T(8,128)(2,1)}), bf16[16,48,256]{2,1,0:T(8,128)(2,1)S(1)}, u32[]{:S(2)}, u32[]{:S(2)}) %all-to-all-start.3) | async-done | bytes 393248 | tf_op jit(solution)/shard_map/all_to_all | solution.py:179
  136.5 0.7 reshape.144
  137.2 6.3 %all-to-all-start.4 = ((f32[16,1,768]{2,1,0:T(1,128)}), f32[16,1,768]{2,1,0:T(1,128)S(1)}, u32[]{:S(2)}, u32[]{:S(2)}) async-start(f32[16,1,768]{2,1,0:T(1,128)} %reshape.144), calls=%async_computation.4 | async-start | bytes 98304 | tf_op jit(solution)/shard_map/all_to_all | solution.py:181
  143.5 0.5 select_reduce_fusion
  144.0 11.2 %all-to-all-done.4 = f32[16,1,768]{2,1,0:T(1,128)S(1)} async-done(((f32[16,1,768]{2,1,0:T(1,128)}), f32[16,1,768]{2,1,0:T(1,128)S(1)}, u32[]{:S(2)}, u32[]{:S(2)}) %all-to-all-start.4) | async-done | bytes 49184 | tf_op jit(solution)/shard_map/all_to_all | solution.py:181
  155.2 0.6 div.45
  (21 shorter events, 0.4 us)
Async XLA Ops:
  1.3 44.6 %all-to-all-start = ((s32[32,1,2]{2,1,0:T(1,128)}), s32[32,1,2]{2,1,0:T(1,128)S(1)}, u32[]{:S(2)}, u32[]{:S(2)}) async-start(s32[32,1,2]{2,1,0:T(1,128)} %broadcast_in_dim.63), calls=%async_computation | async-start | bytes 32768 | tf_op jit(solution)/shard_map/all_to_all | solution.py:160
  104.9 13.5 %copy-start = (bf16[1,768,1024]{2,1,0:T(8,128)(2,1)S(1)}, bf16[1,768,1024]{2,1,0:T(8,128)(2,1)}, u32[]{:S(2)}) copy-start(bf16[1,768,1024]{2,1,0:T(8,128)(2,1)} %forward_ref.1) | copy-start | bytes 4718596
  104.9 13.5 %copy-start.1 = (bf16[1,768,1024]{2,1,0:T(8,128)(2,1)S(1)}, bf16[1,768,1024]{2,1,0:T(8,128)(2,1)}, u32[]{:S(2)}) copy-start(bf16[1,768,1024]{2,1,0:T(8,128)(2,1)} %reversed_ref.1) | copy-start | bytes 4718596
  118.4 9.6 %copy-start.2 = (s32[768,2]{0,1:T(2,128)S(1)}, s32[768,2]{0,1:T(2,128)}, u32[]{:S(2)}) copy-start(s32[768,2]{0,1:T(2,128)} %param.11) | copy-start | bytes 18436
  118.4 9.6 %copy-start.3 = (f32[16]{0:T(128)S(1)}, f32[16]{0:T(128)}, u32[]{:S(2)}) copy-start(f32[16]{0:T(128)} %param.12) | copy-start | bytes 196
  118.5 9.7 %copy-start.4 = (f32[64]{0:T(128)S(1)}, f32[64]{0:T(128)}, u32[]{:S(2)}) copy-start(f32[64]{0:T(128)} %param.13) | copy-start | bytes 772
  120.6 15.8 %all-to-all-start.3 = ((bf16[16,48,256]{2,1,0:T(8,128)(2,1)}), bf16[16,48,256]{2,1,0:T(8,128)(2,1)S(1)}, u32[]{:S(2)}, u32[]{:S(2)}) async-start(bf16[16,48,256]{2,1,0:T(8,128)(2,1)} %residual_terms.1), calls=%async_computation.3 | async-start | bytes 786432 | tf_op jit(solution)/shard_map/all_to_all | solution.py:179
  137.2 18.0 %all-to-all-start.4 = ((f32[16,1,768]{2,1,0:T(1,128)}), f32[16,1,768]{2,1,0:T(1,128)S(1)}, u32[]{:S(2)}, u32[]{:S(2)}) async-start(f32[16,1,768]{2,1,0:T(1,128)} %reshape.144), calls=%async_computation.4 | async-start | bytes 98304 | tf_op jit(solution)/shard_map/all_to_all | solution.py:181

commit v8 on v6

--- a/solution.py
+++ b/solution.py
@@ -15,6 +15,7 @@
 LANES = 128
 PAIRS = BLOCK_VIRTUALS**2
 TOP = 14.0
+QUARTER = GROUP * PAIRS
 
 
 def swap_lane_blocks(tiles):
@@ -54,21 +55,25 @@
     power = jnp.ceil(jnp.log2(jnp.maximum(largest, 2.0**-100)))
     scale = jnp.exp2(TOP - power)
     product_ref[...] = (product * scale).reshape(product_ref.shape)
-    out_ref[:, :, PAIRS:] = jnp.broadcast_to(power, (AW * AW, LANES)).reshape(AW, AW, LANES)
+    out_ref[:, :, QUARTER:] = jnp.broadcast_to(power, (GROUP * AW, LANES)).reshape(GROUP, AW, LANES)
     for c in range(0, BLOCK_VIRTUALS, GROUP):
         for b in range(0, AW, GROUP):
             lanes = slice(b * BLOCK_VIRTUALS, b * BLOCK_VIRTUALS + LANES)
             tiles = [product_ref[:, c + i, lanes] for i in range(GROUP)]
             for j, tile in enumerate(swap_lane_blocks(tiles)):
-                lanes_out = slice(c * BLOCK_VIRTUALS, c * BLOCK_VIRTUALS + LANES)
-                out_ref[b + j, :, lanes_out] = tile
+                at = j * PAIRS + c * BLOCK_VIRTUALS
+                out_ref[b // GROUP, :, at : at + LANES] = tile
 
 
 def select_matmul(hot, rows):
     return jnp.dot(hot, rows, preferred_element_type=jnp.float32).astype(jnp.bfloat16)
 
 
-def residual_kernel(forward_ref, reversed_ref, mirrored_ref, out_ref, term_ref):
+def residual_kernel(forward_ref, reversed_ref, gathered_ref, out_ref, term_ref, mirrored_ref):
+    for b in range(AW):
+        rows = slice(b // GROUP * AW, (b // GROUP + 1) * AW)
+        lanes = slice(b % GROUP * PAIRS, (b % GROUP + 1) * PAIRS)
+        mirrored_ref[b * AW : (b + 1) * AW] = gathered_ref[rows, lanes]
     cells = AW * AW
     row = lax.broadcasted_iota(jnp.int32, (cells, cells), 0)
     col = lax.broadcasted_iota(jnp.int32, (cells, cells), 1)
@@ -97,26 +102,53 @@
         out_ref[at * 2 + 1] = ordered[piece // 2 :]
 
 
-def residual_terms(forward, backward, mirrored):
+def residual_terms(forward, backward, gathered):
     return pl.pallas_call(
         residual_kernel,
         out_shape=jax.ShapeDtypeStruct((16, 48, AW * AW), jnp.bfloat16),
         in_specs=[pl.BlockSpec(memory_space=pltpu.VMEM)] * 3,
         out_specs=pl.BlockSpec(memory_space=pltpu.VMEM),
-        scratch_shapes=[pltpu.VMEM((768, AW * AW), jnp.bfloat16)],
+        scratch_shapes=[
+            pltpu.VMEM((768, AW * AW), jnp.bfloat16),
+            pltpu.VMEM((AW * AW, PAIRS), jnp.bfloat16),
+        ],
         compiler_params=pltpu.CompilerParams(vmem_limit_bytes=24 * 1024 * 1024),
         cost_estimate=pl.CostEstimate(
             flops=4 * 768 * 256 * 1024, bytes_accessed=4 * 1024 * 1024, transcendentals=0
         ),
         name="residual_terms",
-    )(forward, backward, mirrored)
+    )(forward, backward, gathered)
+
+
+def plane_sum_kernel(terms_ref, out_ref, total_ref):
+    total = terms_ref[0].astype(jnp.float32)
+    for source in range(1, 16):
+        total = total + terms_ref[source].astype(jnp.float32)
+    total_ref[...] = total
+    cells = AW * AW
+    for z in range(16):
+        for k in range(3):
+            out_ref[z, :, k * cells : (k + 1) * cells] = total_ref[z * 3 + k : z * 3 + k + 1]
+
+
+def plane_sums(terms):
+    return pl.pallas_call(
+        plane_sum_kernel,
+        out_shape=jax.ShapeDtypeStruct((16, 1, 768), jnp.float32),
+        in_specs=[pl.BlockSpec(memory_space=pltpu.VMEM)],
+        out_specs=pl.BlockSpec(memory_space=pltpu.VMEM),
+        scratch_shapes=[pltpu.VMEM((48, AW * AW), jnp.float32)],
+        compiler_params=pltpu.CompilerParams(vmem_limit_bytes=8 * 1024 * 1024),
+        cost_estimate=pl.CostEstimate(flops=16 * 48 * 256, bytes_accessed=442368, transcendentals=0),
+        name="plane_sums",
+    )(terms)
 
 
 def block_integrals(picked):
     side = AW * BLOCK_VIRTUALS
     return pl.pallas_call(
         integrals_kernel,
-        out_shape=jax.ShapeDtypeStruct((AW, AW, PAIRS + LANES), jnp.float32),
+        out_shape=jax.ShapeDtypeStruct((GROUP, AW, QUARTER + LANES), jnp.float32),
         in_specs=[pl.BlockSpec(memory_space=pltpu.VMEM)],
         out_specs=pl.BlockSpec(memory_space=pltpu.VMEM),
         scratch_shapes=[
@@ -165,15 +197,15 @@
     picked = select_rows(one_hot_rows(wanted, NV), line)
     picked = picked.reshape(16, 2 * BLOCK_VIRTUALS, AW * q_line)
     picked = lax.all_to_all(picked, PLANE, 0, 0, tiled=True)
-    partial_sum = block_integrals(picked).astype(jnp.float16).reshape(4, 4 * AW, -1)
+    partial_sum = block_integrals(picked).astype(jnp.float16)
     quarters = lax.all_to_all(partial_sum, "yh", 0, 0, tiled=True)
     quarters = quarters.astype(jnp.float32)
-    unscale = jnp.exp2(quarters[:, :1, PAIRS : PAIRS + 1] - TOP)
-    coulomb = jnp.sum(quarters[:, :, :PAIRS] * unscale, axis=0)
-    mirrored = lax.all_gather(coulomb.astype(jnp.bfloat16), "yh", axis=0, tiled=True)
-    ordered = residual_terms(amplitude_forward, amplitude_reversed, mirrored)
+    unscale = jnp.exp2(quarters[:, :1, QUARTER : QUARTER + 1] - TOP)
+    coulomb = jnp.sum(quarters[:, :, :QUARTER] * unscale, axis=0)
+    gathered = lax.all_gather(coulomb.astype(jnp.bfloat16), "yh", axis=0, tiled=True)
+    ordered = residual_terms(amplitude_forward, amplitude_reversed, gathered)
     ordered = lax.all_to_all(ordered, PLANE, 0, 0, tiled=True)
-    plane_sum = jnp.sum(ordered.astype(jnp.float32), axis=0).reshape(16, 1, 768)
+    plane_sum = plane_sums(ordered)
     owned = jnp.sum(lax.all_to_all(plane_sum, "z", 0, 0, tiled=True), axis=0)
 
     owned_len = owned.shape[1]

time: 153 us -> 152 us (level)
  no operation moved by 1% of the time
where the time goes in v8:
time: 152 us
  blocking collectives  92.4 us (61%)
  starting transfers between devices  30.4 us (20%)
  waiting for transfers between devices  19 us (12%)
  Pallas kernels  5.07 us (3%)
  local copies, waits for them, and re-layouts  2.27 us (1%)
    all_gather x1, blocking collectives, shards(): line = lax.all_gather(factor, 'z', axis=0, tiled=True)  29.6 us
    all_to_all x1, blocking collectives, shards(): picked = lax.all_to_all(picked, PLANE, 0, 0, tiled=True)  28.1 us
    all_to_all x1, blocking collectives, shards(): quarters = lax.all_to_all(partial_sum, 'yh', 0, 0, tiled=True)  19.4 us
    all_to_all x1, starting transfers between devices, shards(): lax.all_to_all(jnp.broadcast_to(block_map, (16, 2)), PLANE, 0, 0, tiled=T...  17.4 us
    all_gather x1, blocking collectives, shards(): lax.all_gather(coulomb.astype(jnp.bfloat16), 'yh', axis=0, tiled=True)  15.3 us
    all_to_all x1, waiting for transfers between devices, shards(): owned = jnp.sum(lax.all_to_all(plane_sum, 'z', 0, 0, tiled=True), axis=0)  10.9 us
    all_to_all x1, starting transfers between devices, shards(): ordered = lax.all_to_all(ordered, PLANE, 0, 0, tiled=True)  9.43 us
    all_to_all x1, waiting for transfers between devices, shards(): ordered = lax.all_to_all(ordered, PLANE, 0, 0, tiled=True)  8.08 us
  transfers between devices with their start and end apart: 3, of which 2 were waited for; matrix products, arithmetic and copies ran while one was open for 1% of the time, Pallas kernels for 0%

profile of v8, /device:TPU:1, one launch (start us, length us, event | category | flops | bytes accessed | tf_op | source)
XLA Modules:
  0.0 151.5 jit_solution(1295988873099867235)
XLA Ops:
  0.0 1.3 broadcast_in_dim.63
  1.3 17.4 %all-to-all-start = ((s32[16,1,2]{2,1,0:T(1,128)}), s32[16,1,2]{2,1,0:T(1,128)S(1)}, u32[]{:S(2)}, u32[]{:S(2)}) async-start(s32[16,1,2]{2,1,0:T(1,128)} %broadcast_in_dim.63), calls=%async_computation | async-start | bytes 16384 | tf_op jit(solution)/shard_map/all_to_all | solution.py:188
  18.7 29.6 %all_gather.6 = bf16[32,16,704]{2,1,0:T(8,128)(2,1)S(1)} all-gather(bf16[2,16,704]{2,1,0:T(8,128)(2,1)} %param.7), channel_id=1, replica_groups=mesh['yl'=2,'x'=4,'z'=16,'core'=2,'yh'=4] {'z'}, dimensions={0}, use_global_device_ids=true | all-gather | bytes 765952 | tf_op jit(solution)/shard_map/all_gather | solution.py:191
  48.3 0.2 copy.10
  48.5 0.1 mul.38
  48.6 0.1 iota_add_fusion
  48.7 0.1 add.87
  48.8 1.0 fusion.2
  49.8 28.1 %all_to_all.26.picked_ref = bf16[16,64,512]{2,1,0:T(8,128)(2,1)S(1)} all-to-all(bf16[16,64,512]{2,1,0:T(8,128)(2,1)S(1)} %bitcast.6), channel_id=1, replica_groups=mesh['yl'=2,'x'=4,'z'=16,'core'=2,'yh'=4] {'yl','x','core'}, dimensions={0} | all-to-all | bytes 2097152 | tf_op jit(solution)/shard_map/all_to_all | solution.py:199
  77.9 2.3 %block_integrals.1 = f32[4,16,4224]{2,1,0:T(8,128)S(1)} custom-call(bf16[16,64,512]{2,1,0:T(8,128)(2,1)S(1)} %all_to_all.26.picked_ref), custom_call_target="tpu_custom_call" | custom-call | flops 268435456 | bytes 2097152 | tf_op jit(solution)/shard_map/block_integrals/pallas_call | solution.py:149
  80.2 19.4 %all_to_all.27 = f16[4,16,4224]{2,1,0:T(8,128)(2,1)S(1)} all-to-all(f16[4,16,4224]{2,1,0:T(8,128)(2,1)S(1)} %convert_element_type.14), channel_id=1, replica_groups=mesh['yl'=2,'x'=4,'z'=16,'core'=2,'yh'=4] {'yh'}, dimensions={0} | all-to-all | bytes 1081344 | tf_op jit(solution)/shard_map/all_to_all | solution.py:201
  99.7 0.1 fusion.13
  99.8 0.1 fusion.3
  100.0 15.3 %all_gather.7.gathered_ref = bf16[64,4096]{1,0:T(8,128)(2,1)S(1)} all-gather(bf16[16,4096]{1,0:T(8,128)(2,1)S(1)} %fusion.3), channel_id=1, replica_groups=mesh['yl'=2,'x'=4,'z'=16,'core'=2,'yh'=4] {'yh'}, dimensions={0}, use_global_device_ids=true | all-gather | bytes 655360 | tf_op jit(solution)/shard_map/all_gather | solution.py:205
  115.3 2.1 %residual_terms.1 = bf16[16,48,256]{2,1,0:T(8,128)(2,1)} custom-call(bf16[1,768,1024]{2,1,0:T(8,128)(2,1)S(1)} %copy-done, bf16[1,768,1024]{2,1,0:T(8,128)(2,1)S(1)} %copy-done.1, bf16[64,4096]{1,0:T(8,128)(2,1)S(1)} %all_gather.7.gathered_ref), custom_call_target="tpu_custom_call" | custom-call | flops 805306368 | bytes 4194304 | tf_op jit(solution)/shard_map/residual_terms/pallas_call | solution.py:106
  117.4 9.4 %all-to-all-start.3 = ((bf16[16,48,256]{2,1,0:T(8,128)(2,1)}), bf16[16,48,256]{2,1,0:T(8,128)(2,1)S(1)}, u32[]{:S(2)}, u32[]{:S(2)}) async-start(bf16[16,48,256]{2,1,0:T(8,128)(2,1)} %residual_terms.1), calls=%async_computation.3 | async-start | bytes 786432 | tf_op jit(solution)/shard_map/all_to_all | solution.py:207
  126.9 0.1 select_reduce_fusion.4
  127.0 0.1 select_reduce_fusion.1
  127.2 8.1 %all-to-all-done.3.terms_ref = bf16[16,48,256]{2,1,0:T(8,128)(2,1)S(1)} async-done(((bf16[16,48,256]{2,1,0:T(8,128)(2,1)}), bf16[16,48,256]{2,1,0:T(8,128)(2,1)S(1)}, u32[]{:S(2)}, u32[]{:S(2)}) %all-to-all-start.3) | async-done | bytes 393248 | tf_op jit(solution)/shard_map/all_to_all | solution.py:207
  135.3 0.7 plane_sums.1
  136.0 3.5 %all-to-all-start.4 = ((f32[16,1,768]{2,1,0:T(1,128)}), f32[16,1,768]{2,1,0:T(1,128)S(1)}, u32[]{:S(2)}, u32[]{:S(2)}) async-start(f32[16,1,768]{2,1,0:T(1,128)} %plane_sums.1), calls=%async_computation.4 | async-start | bytes 98304 | tf_op jit(solution)/shard_map/all_to_all | solution.py:209
  139.5 0.5 select_reduce_fusion
  140.0 10.9 %all-to-all-done.4 = f32[16,1,768]{2,1,0:T(1,128)S(1)} async-done(((f32[16,1,768]{2,1,0:T(1,128)}), f32[16,1,768]{2,1,0:T(1,128)S(1)}, u32[]{:S(2)}, u32[]{:S(2)}) %all-to-all-start.4) | async-done | bytes 49184 | tf_op jit(solution)/shard_map/all_to_all | solution.py:209
  151.0 0.6 div.45
  (20 shorter events, 0.3 us)
Async XLA Ops:
  1.3 47.3 %all-to-all-start = ((s32[16,1,2]{2,1,0:T(1,128)}), s32[16,1,2]{2,1,0:T(1,128)S(1)}, u32[]{:S(2)}, u32[]{:S(2)}) async-start(s32[16,1,2]{2,1,0:T(1,128)} %broadcast_in_dim.63), calls=%async_computation | async-start | bytes 16384 | tf_op jit(solution)/shard_map/all_to_all | solution.py:188
  99.6 15.7 %copy-start = (bf16[1,768,1024]{2,1,0:T(8,128)(2,1)S(1)}, bf16[1,768,1024]{2,1,0:T(8,128)(2,1)}, u32[]{:S(2)}) copy-start(bf16[1,768,1024]{2,1,0:T(8,128)(2,1)} %forward_ref.1) | copy-start | bytes 4718596
  99.6 15.7 %copy-start.1 = (bf16[1,768,1024]{2,1,0:T(8,128)(2,1)S(1)}, bf16[1,768,1024]{2,1,0:T(8,128)(2,1)}, u32[]{:S(2)}) copy-start(bf16[1,768,1024]{2,1,0:T(8,128)(2,1)} %reversed_ref.1) | copy-start | bytes 4718596
  115.3 11.6 %copy-start.2 = (s32[768,2]{0,1:T(2,128)S(1)}, s32[768,2]{0,1:T(2,128)}, u32[]{:S(2)}) copy-start(s32[768,2]{0,1:T(2,128)} %param.11) | copy-start | bytes 18436
  115.3 11.6 %copy-start.3 = (f32[16]{0:T(128)S(1)}, f32[16]{0:T(128)}, u32[]{:S(2)}) copy-start(f32[16]{0:T(128)} %param.12) | copy-start | bytes 196
  115.3 11.7 %copy-start.4 = (f32[64]{0:T(128)S(1)}, f32[64]{0:T(128)}, u32[]{:S(2)}) copy-start(f32[64]{0:T(128)} %param.13) | copy-start | bytes 772
  117.4 17.8 %all-to-all-start.3 = ((bf16[16,48,256]{2,1,0:T(8,128)(2,1)}), bf16[16,48,256]{2,1,0:T(8,128)(2,1)S(1)}, u32[]{:S(2)}, u32[]{:S(2)}) async-start(bf16[16,48,256]{2,1,0:T(8,128)(2,1)} %residual_terms.1), calls=%async_computation.3 | async-start | bytes 786432 | tf_op jit(solution)/shard_map/all_to_all | solution.py:207
  136.0 14.9 %all-to-all-start.4 = ((f32[16,1,768]{2,1,0:T(1,128)}), f32[16,1,768]{2,1,0:T(1,128)S(1)}, u32[]{:S(2)}, u32[]{:S(2)}) async-start(f32[16,1,768]{2,1,0:T(1,128)} %plane_sums.1), calls=%async_computation.4 | async-start | bytes 98304 | tf_op jit(solution)/shard_map/all_to_all | solution.py:209

commit v9 on v8

--- a/solution.py
+++ b/solution.py
@@ -11,6 +11,7 @@
 NV = 704
 BLK = ("yl", "x", "z", "core")
 PLANE = ("yl", "x", "core")
+SPREAD = ("x", "yl", "core")
 GROUP = 4
 LANES = 128
 PAIRS = BLOCK_VIRTUALS**2
@@ -186,7 +187,7 @@
     factor, amplitude_forward, amplitude_reversed, block_map, pair_list, virt_energy, occ_energy
 ):
     plane_map = lax.all_to_all(
-        jnp.broadcast_to(block_map, (16, 2)), PLANE, 0, 0, tiled=True
+        jnp.broadcast_to(block_map, (16, 2)), SPREAD, 0, 0, tiled=True
     )
     line = lax.all_gather(factor, "z", axis=0, tiled=True)
     q_line = line.shape[0]
@@ -196,7 +197,7 @@
     line = line.transpose(1, 0, 2).reshape(AW * q_line, NV)
     picked = select_rows(one_hot_rows(wanted, NV), line)
     picked = picked.reshape(16, 2 * BLOCK_VIRTUALS, AW * q_line)
-    picked = lax.all_to_all(picked, PLANE, 0, 0, tiled=True)
+    picked = lax.all_to_all(picked, SPREAD, 0, 0, tiled=True)
     partial_sum = block_integrals(picked).astype(jnp.float16)
     quarters = lax.all_to_all(partial_sum, "yh", 0, 0, tiled=True)
     quarters = quarters.astype(jnp.float32)

time: 152 us -> 152 us (level)
  starting transfers between devices: 30.4 us -> 33.2 us
  blocking collectives: 92.4 us -> 90 us
    all_to_all x1, starting transfers between devices: 9.43 us -> 12.2 us  [shards(): ordered = lax.all_to_all(ordered, PLANE, 0, 0, tiled=True)]
where the time goes in v9:
time: 152 us
  blocking collectives  90 us (59%)
  starting transfers between devices  33.2 us (22%)
  waiting for transfers between devices  19.1 us (13%)
  Pallas kernels  5.07 us (3%)
  local copies, waits for them, and re-layouts  2.27 us (1%)
    all_gather x1, blocking collectives, shards(): line = lax.all_gather(factor, 'z', axis=0, tiled=True)  29.6 us
    all_to_all x1, blocking collectives, shards(): picked = lax.all_to_all(picked, SPREAD, 0, 0, tiled=True)  28.1 us
    all_to_all x1, blocking collectives, shards(): quarters = lax.all_to_all(partial_sum, 'yh', 0, 0, tiled=True)  18.5 us
    all_to_all x1, starting transfers between devices, shards(): lax.all_to_all(jnp.broadcast_to(block_map, (16, 2)), SPREAD, 0, 0, tiled=...  17.4 us
    all_gather x1, blocking collectives, shards(): lax.all_gather(coulomb.astype(jnp.bfloat16), 'yh', axis=0, tiled=True)  13.9 us
    all_to_all x1, starting transfers between devices, shards(): ordered = lax.all_to_all(ordered, PLANE, 0, 0, tiled=True)  12.2 us
    all_to_all x1, waiting for transfers between devices, shards(): owned = jnp.sum(lax.all_to_all(plane_sum, 'z', 0, 0, tiled=True), axis=0)  11 us
    all_to_all x1, waiting for transfers between devices, shards(): ordered = lax.all_to_all(ordered, PLANE, 0, 0, tiled=True)  8.16 us
  transfers between devices with their start and end apart: 3, of which 2 were waited for; matrix products, arithmetic and copies ran while one was open for 1% of the time, Pallas kernels for 0%

profile of v9, /device:TPU:1, one launch (start us, length us, event | category | flops | bytes accessed | tf_op | source)
XLA Modules:
  0.0 152.1 jit_solution(8003074617750292377)
XLA Ops:
  0.0 1.3 broadcast_in_dim.63
  1.3 17.4 %all-to-all-start = ((s32[16,1,2]{2,1,0:T(1,128)}), s32[16,1,2]{2,1,0:T(1,128)S(1)}, u32[]{:S(2)}, u32[]{:S(2)}) async-start(s32[16,1,2]{2,1,0:T(1,128)} %broadcast_in_dim.63), calls=%async_computation | async-start | bytes 16384 | tf_op jit(solution)/shard_map/all_to_all | solution.py:189
  18.7 29.6 %all_gather.6 = bf16[32,16,704]{2,1,0:T(8,128)(2,1)S(1)} all-gather(bf16[2,16,704]{2,1,0:T(8,128)(2,1)} %param.7), channel_id=1, replica_groups=mesh['yl'=2,'x'=4,'z'=16,'core'=2,'yh'=4] {'z'}, dimensions={0}, use_global_device_ids=true | all-gather | bytes 765952 | tf_op jit(solution)/shard_map/all_gather | solution.py:192
  48.3 0.2 copy.10
  48.5 0.1 mul.38
  48.6 0.1 iota_add_fusion
  48.7 0.1 add.87
  48.8 1.0 fusion.2
  49.8 28.1 %all_to_all.26.picked_ref = bf16[16,64,512]{2,1,0:T(8,128)(2,1)S(1)} all-to-all(bf16[16,64,512]{2,1,0:T(8,128)(2,1)S(1)} %bitcast.6), channel_id=1, replica_groups=mesh['yl'=2,'x'=4,'z'=16,'core'=2,'yh'=4] {'x','yl','core'}, dimensions={0} | all-to-all | bytes 2097152 | tf_op jit(solution)/shard_map/all_to_all | solution.py:200
  77.9 2.3 %block_integrals.1 = f32[4,16,4224]{2,1,0:T(8,128)S(1)} custom-call(bf16[16,64,512]{2,1,0:T(8,128)(2,1)S(1)} %all_to_all.26.picked_ref), custom_call_target="tpu_custom_call" | custom-call | flops 268435456 | bytes 2097152 | tf_op jit(solution)/shard_map/block_integrals/pallas_call | solution.py:150
  80.2 18.5 %all_to_all.27 = f16[4,16,4224]{2,1,0:T(8,128)(2,1)S(1)} all-to-all(f16[4,16,4224]{2,1,0:T(8,128)(2,1)S(1)} %convert_element_type.14), channel_id=1, replica_groups=mesh['yl'=2,'x'=4,'z'=16,'core'=2,'yh'=4] {'yh'}, dimensions={0} | all-to-all | bytes 1081344 | tf_op jit(solution)/shard_map/all_to_all | solution.py:202
  98.8 0.1 fusion.13
  98.9 0.1 fusion.3
  99.0 13.9 %all_gather.7.gathered_ref = bf16[64,4096]{1,0:T(8,128)(2,1)S(1)} all-gather(bf16[16,4096]{1,0:T(8,128)(2,1)S(1)} %fusion.3), channel_id=1, replica_groups=mesh['yl'=2,'x'=4,'z'=16,'core'=2,'yh'=4] {'yh'}, dimensions={0}, use_global_device_ids=true | all-gather | bytes 655360 | tf_op jit(solution)/shard_map/all_gather | solution.py:206
  112.9 2.1 %residual_terms.1 = bf16[16,48,256]{2,1,0:T(8,128)(2,1)} custom-call(bf16[1,768,1024]{2,1,0:T(8,128)(2,1)S(1)} %copy-done, bf16[1,768,1024]{2,1,0:T(8,128)(2,1)S(1)} %copy-done.1, bf16[64,4096]{1,0:T(8,128)(2,1)S(1)} %all_gather.7.gathered_ref), custom_call_target="tpu_custom_call" | custom-call | flops 805306368 | bytes 4194304 | tf_op jit(solution)/shard_map/residual_terms/pallas_call | solution.py:107
  115.0 12.2 %all-to-all-start.3 = ((bf16[16,48,256]{2,1,0:T(8,128)(2,1)}), bf16[16,48,256]{2,1,0:T(8,128)(2,1)S(1)}, u32[]{:S(2)}, u32[]{:S(2)}) async-start(bf16[16,48,256]{2,1,0:T(8,128)(2,1)} %residual_terms.1), calls=%async_computation.3 | async-start | bytes 786432 | tf_op jit(solution)/shard_map/all_to_all | solution.py:208
  127.3 0.1 select_reduce_fusion.4
  127.4 0.1 select_reduce_fusion.1
  127.6 8.2 %all-to-all-done.3.terms_ref = bf16[16,48,256]{2,1,0:T(8,128)(2,1)S(1)} async-done(((bf16[16,48,256]{2,1,0:T(8,128)(2,1)}), bf16[16,48,256]{2,1,0:T(8,128)(2,1)S(1)}, u32[]{:S(2)}, u32[]{:S(2)}) %all-to-all-start.3) | async-done | bytes 393248 | tf_op jit(solution)/shard_map/all_to_all | solution.py:208
  135.7 0.7 plane_sums.1
  136.4 3.5 %all-to-all-start.4 = ((f32[16,1,768]{2,1,0:T(1,128)}), f32[16,1,768]{2,1,0:T(1,128)S(1)}, u32[]{:S(2)}, u32[]{:S(2)}) async-start(f32[16,1,768]{2,1,0:T(1,128)} %plane_sums.1), calls=%async_computation.4 | async-start | bytes 98304 | tf_op jit(solution)/shard_map/all_to_all | solution.py:210
  140.0 0.5 select_reduce_fusion
  140.4 11.0 %all-to-all-done.4 = f32[16,1,768]{2,1,0:T(1,128)S(1)} async-done(((f32[16,1,768]{2,1,0:T(1,128)}), f32[16,1,768]{2,1,0:T(1,128)S(1)}, u32[]{:S(2)}, u32[]{:S(2)}) %all-to-all-start.4) | async-done | bytes 49184 | tf_op jit(solution)/shard_map/all_to_all | solution.py:210
  151.5 0.6 div.45
  (20 shorter events, 0.3 us)
Async XLA Ops:
  1.3 47.3 %all-to-all-start = ((s32[16,1,2]{2,1,0:T(1,128)}), s32[16,1,2]{2,1,0:T(1,128)S(1)}, u32[]{:S(2)}, u32[]{:S(2)}) async-start(s32[16,1,2]{2,1,0:T(1,128)} %broadcast_in_dim.63), calls=%async_computation | async-start | bytes 16384 | tf_op jit(solution)/shard_map/all_to_all | solution.py:189
  98.7 14.2 %copy-start = (bf16[1,768,1024]{2,1,0:T(8,128)(2,1)S(1)}, bf16[1,768,1024]{2,1,0:T(8,128)(2,1)}, u32[]{:S(2)}) copy-start(bf16[1,768,1024]{2,1,0:T(8,128)(2,1)} %forward_ref.1) | copy-start | bytes 4718596
  98.7 14.2 %copy-start.1 = (bf16[1,768,1024]{2,1,0:T(8,128)(2,1)S(1)}, bf16[1,768,1024]{2,1,0:T(8,128)(2,1)}, u32[]{:S(2)}) copy-start(bf16[1,768,1024]{2,1,0:T(8,128)(2,1)} %reversed_ref.1) | copy-start | bytes 4718596
  112.9 14.4 %copy-start.2 = (s32[768,2]{0,1:T(2,128)S(1)}, s32[768,2]{0,1:T(2,128)}, u32[]{:S(2)}) copy-start(s32[768,2]{0,1:T(2,128)} %param.11) | copy-start | bytes 18436
  112.9 14.4 %copy-start.3 = (f32[16]{0:T(128)S(1)}, f32[16]{0:T(128)}, u32[]{:S(2)}) copy-start(f32[16]{0:T(128)} %param.12) | copy-start | bytes 196
  112.9 14.5 %copy-start.4 = (f32[64]{0:T(128)S(1)}, f32[64]{0:T(128)}, u32[]{:S(2)}) copy-start(f32[64]{0:T(128)} %param.13) | copy-start | bytes 772
  115.0 20.7 %all-to-all-start.3 = ((bf16[16,48,256]{2,1,0:T(8,128)(2,1)}), bf16[16,48,256]{2,1,0:T(8,128)(2,1)S(1)}, u32[]{:S(2)}, u32[]{:S(2)}) async-start(bf16[16,48,256]{2,1,0:T(8,128)(2,1)} %residual_terms.1), calls=%async_computation.3 | async-start | bytes 786432 | tf_op jit(solution)/shard_map/all_to_all | solution.py:208
  136.4 15.0 %all-to-all-start.4 = ((f32[16,1,768]{2,1,0:T(1,128)}), f32[16,1,768]{2,1,0:T(1,128)S(1)}, u32[]{:S(2)}, u32[]{:S(2)}) async-start(f32[16,1,768]{2,1,0:T(1,128)} %plane_sums.1), calls=%async_computation.4 | async-start | bytes 98304 | tf_op jit(solution)/shard_map/all_to_all | solution.py:210
